TPU v7x, 512 devices: a whole 4x8x8 slice. The times are simulated.
512 devices in a mesh: beam: 64 (over x, z, core), head: 8 (over y).
Axes of the slice: x: 4, y: 8, z: 8, core: 2. Of those that a mesh axis runs over, the one named last changes fastest.
Arguments:
- queries: bfloat16 [256, 8192], P('beam', 'head')
- new_keys: bfloat16 [256, 1024], P('beam', 'head')
- new_values: bfloat16 [256, 1024], P('beam', 'head'), may hold values from -6 to 6
- prompt_keys: bfloat16 [16, 16384, 1024], P(None, 'beam', 'head')
- prompt_values: bfloat16 [16, 16384, 1024], P(None, 'beam', 'head'), may hold values from -6 to 6
- private_keys: bfloat16 [256, 512, 1024], P('beam', None, 'head'), may hold values from -16 to 16
- private_values: bfloat16 [256, 512, 1024], P('beam', None, 'head'), may hold values from -6 to 6
- parents: int32 [256], P('beam'), may hold values from 0 to 255, as said below
- block_counts: int32 [256], P('beam'), may hold values from 1 to 4
- out_weight: bfloat16 [8192, 8192], P('head', 'beam'), may hold values from -0.0625 to 0.0625
Outputs:
- mixed: bfloat16 [256, 8192], P('head', 'beam')
Inputs may be any that keep to these rules, and one draw needn't show every extreme that they name: Every beam's parent belongs to the same request: parents[b] // 16 == b // 16.
All inputs are finite; a program needn't handle non-finite values.
Results may differ from a plain program's by a relative error of at most 0.0049.
Values may be sent and summed in bfloat16 or wider, within the bound.
A program may use at most 64 MiB of HBM per device.

v0:
```python
import math

import jax
import jax.numpy as jnp
from jax import lax
from jax.sharding import PartitionSpec as P

HD = 128
QPK = 8
BEAM_WIDTH = 16
BLOCK_LEN = 128


masked_score = -1e30


def shifted(x, axis, by):
    length = lax.axis_size(axis)
    pairs = [(i, i + by) for i in range(length) if 0 <= i + by < length]
    return lax.ppermute(x, axis, pairs)


def suffix_part(query_head_count, cache_keys, cache_values, counts):
    beams = cache_keys.shape[0]
    length = cache_keys.shape[1]
    heads = query_head_count.shape[1]
    key_heads = cache_keys.reshape(beams, length, heads, HD)
    value_heads = cache_values.reshape(beams, length, heads, HD)
    scores = jnp.einsum(
        "bkqd,bpkd->bkqp", query_head_count, key_heads, preferred_element_type=jnp.float32
    ) * (1.0 / math.sqrt(HD))
    allowed = lax.broadcasted_iota(jnp.int32, (beams, length), 1) < (counts * BLOCK_LEN)[:, None]
    scores = jnp.where(allowed[:, None, None, :], scores, masked_score)
    highest = jnp.max(scores, axis=-1)
    weights = jnp.exp(scores - highest[..., None])
    totals = jnp.sum(weights, axis=-1)
    summed = jnp.einsum(
        "bkqp,bpkd->bkqd",
        weights.astype(jnp.bfloat16),
        value_heads,
        preferred_element_type=jnp.float32,
    )
    return (summed, highest, totals)


def per_device(
    queries,
    new_keys,
    new_values,
    prompt_keys,
    prompt_values,
    private_keys,
    private_values,
    parents,
    block_counts,
    out_weight,
):
    local_beams = queries.shape[0]
    local_heads = new_keys.shape[1] // HD
    token_position = lax.axis_index("beam")
    group = BEAM_WIDTH // local_beams
    logit_scale = 1.0 / math.sqrt(HD)
    query_head_count = queries.reshape(local_beams, local_heads, QPK, HD)
    everyone = lax.all_gather(queries, "beam", axis=0, tiled=True)
    requests = prompt_keys.shape[0]
    prompt_len = prompt_keys.shape[1]
    all_beams = requests * BEAM_WIDTH
    query_groups = everyone.reshape(requests, BEAM_WIDTH, local_heads, QPK, HD)
    prompt_heads = prompt_keys.reshape(requests, prompt_len, local_heads, HD)
    prompt_vals = prompt_values.reshape(requests, prompt_len, local_heads, HD)
    scores = (
        jnp.einsum(
            "rbkqd,rtkd->rbkqt", query_groups, prompt_heads, preferred_element_type=jnp.float32
        )
        * logit_scale
    )
    local_max = jnp.max(scores, axis=-1)
    prompt_max = lax.pmax(local_max, "beam")
    weights = jnp.exp(scores - prompt_max[..., None])
    totals = jnp.sum(weights, axis=-1)
    summed = jnp.einsum(
        "rbkqt,rtkd->rbkqd",
        weights.astype(jnp.bfloat16),
        prompt_vals,
        preferred_element_type=jnp.float32,
    )
    prompt_num, prompt_denominator = (
        lax.psum_scatter(summed.reshape(all_beams, -1), "beam", scatter_dimension=0, tiled=True),
        lax.psum_scatter(totals.reshape(all_beams, -1), "beam", scatter_dimension=0, tiled=True),
    )
    prompt_num = prompt_num.reshape(local_beams, local_heads, QPK, HD)
    prompt_denominator = prompt_denominator.reshape(local_beams, local_heads, QPK)
    own_max = lax.dynamic_slice_in_dim(
        prompt_max.reshape(all_beams, local_heads, QPK),
        token_position * local_beams,
        local_beams,
        0,
    )
    holder = parents // local_beams - token_position
    moved_keys = private_keys
    moved_values = private_values
    shifted_count_totals = block_counts
    for offset in range(1 - group, group):
        chosen = holder == offset
        if offset == 0:
            source = (private_keys, private_values, block_counts)
        else:
            arrived = shifted(
                (private_keys, private_values, block_counts.astype(jnp.bfloat16)), "beam", -offset
            )
            source = (arrived[0], arrived[1], arrived[2].astype(jnp.int32))
        picked_rows = jnp.clip(
            parents - (token_position + offset) * local_beams, 0, local_beams - 1
        )
        moved_keys = jnp.where(
            chosen[:, None, None], jnp.take(source[0], picked_rows, axis=0), moved_keys
        )
        moved_values = jnp.where(
            chosen[:, None, None], jnp.take(source[1], picked_rows, axis=0), moved_values
        )
        shifted_count_totals = jnp.where(
            chosen, jnp.take(source[2], picked_rows), shifted_count_totals
        )
    suffix_num, suffix_max, suffix_den = suffix_part(
        query_head_count, moved_keys, moved_values, shifted_count_totals
    )
    fresh_head_rows = new_keys.reshape(local_beams, local_heads, HD)
    beam_self_logit = (
        jnp.einsum(
            "sxjr,sxr->sxj", query_head_count, fresh_head_rows, preferred_element_type=jnp.float32
        )
        * logit_scale
    )
    overall = jnp.maximum(jnp.maximum(own_max, suffix_max), beam_self_logit)
    first = jnp.exp(own_max - overall)
    second = jnp.exp(suffix_max - overall)
    third = jnp.exp(beam_self_logit - overall)
    own_values = new_values.reshape(local_beams, local_heads, 1, HD).astype(jnp.float32)
    numer = (
        first[..., None] * prompt_num
        + second[..., None] * suffix_num
        + third[..., None] * own_values
    )
    denom = first * prompt_denominator + second * suffix_den + third
    attended = (numer / denom[..., None]).astype(jnp.bfloat16).reshape(local_beams, -1)
    products = jnp.dot(
        lax.all_gather(attended, "beam", axis=0, tiled=True),
        out_weight,
        preferred_element_type=jnp.float32,
    )
    return lax.psum_scatter(products, "head", scatter_dimension=0, tiled=True).astype(jnp.bfloat16)


def solution(mesh):
    placed = (
        P("beam", "head"),
        P("beam", "head"),
        P("beam", "head"),
        P(None, "beam", "head"),
        P(None, "beam", "head"),
        P("beam", None, "head"),
        P("beam", None, "head"),
        P("beam"),
        P("beam"),
        P("head", "beam"),
    )
    return jax.shard_map(
        per_device, mesh=mesh, in_specs=placed, out_specs=P("head", "beam"), check_vma=False
    )
```

profile of v0, /device:TPU:1, one launch (start us, length us, event | category | flops | bytes accessed | tf_op | source)
XLA Modules:
  0.0 780.1 jit_solution(6810854498030112153)
XLA Ops:
  6.5 1.3 convert_element_type.44
  7.8 1.3 collective-permute-start.1
  9.1 8.8 %collective-permute-start.2 = (bf16[4]{0:T(256)(128)(2,1)}, bf16[4]{0:T(256)(128)(2,1)}, u32[]{:S(2)}, u32[]{:S(2)}) collective-permute-start(bf16[4]{0:T(256)(128)(2,1)} %convert_element_type.44), channel_id=1, source_target_pairs={{8,0},{16,8},{24,16},{32,24},{40,32},{48,40},{56,48},{64,56},{72,6... | collective-permute-start | bytes 32 | tf_op jit(solution)/shard_map/ppermute | solution.py:20
  17.9 4.2 collective-permute-start.3
  22.1 1.3 collective-permute-start.7
  23.4 1.9 collective-permute-start.8
  25.3 65.4 %all-gather = bf16[64,4,1024]{2,1,0:T(4,128)(2,1)S(1)} all-gather(bf16[1,4,1024]{2,1,0:T(4,128)(2,1)} %bitcast.116), channel_id=1, replica_groups=mesh['beam'=64,'head'=8] {'beam'}, dimensions={0}, use_global_device_ids=true | all-gather | bytes 532480 | tf_op jit(solution)/shard_map/all_gather | solution.py:64
  90.7 1.0 reshape.135
  91.7 1.6 bitcast_reduce_fusion
  93.2 243.2 %pmax.7 = f32[16,16,1,8]{1,3,0,2:T(8,128)S(1)} all-reduce(f32[16,16,1,8]{1,3,0,2:T(8,128)S(1)} %bitcast.113), channel_id=1, replica_groups=mesh['beam'=64,'head'=8] {'beam'}, use_global_device_ids=true, to_apply=%region_1.0 | all-reduce | flops 2048 | bytes 16384 | tf_op jit(solution)/shard_map/pmax | solution.py:78
  336.5 0.7 fusion.1
  338.3 1.2 copy.53
  340.2 1.1 gather_fusion.3
  341.4 1.4 gather_fusion.10
  343.0 0.6 gather_fusion.17
  344.2 1.3 dynamic-slice
  346.1 246.4 %all-reduce.1 = f32[256,8]{1,0:T(8,128)S(1)} all-reduce(f32[256,8]{1,0:T(8,128)S(1)} %bitcast.112), channel_id=3, replica_groups=mesh['beam'=64,'head'=8] {'beam'}, use_global_device_ids=true, to_apply=%region_5.8.clone | all-reduce | flops 2048 | bytes 16384
  592.5 1.3 collective-permute-start.4
  593.8 1.3 collective-permute-start.5
  595.1 1.3 collective-permute-start
  596.4 8.1 %collective-permute-start.9 = (bf16[4,512,128]{2,1,0:T(8,128)(2,1)S(1)}, bf16[4,512,128]{2,1,0:T(8,128)(2,1)S(1)}, u32[]{:S(2)}, u32[]{:S(2)}) collective-permute-start(bf16[4,512,128]{2,1,0:T(8,128)(2,1)S(1)} %copy-done.3), channel_id=1, source_target_pairs={{0,8},{8,16},{16,24},{24,32},{32,40},{40,48},{48,56},{56,64},{64,7... | collective-permute-start | bytes 1572872 | tf_op jit(solution)/shard_map/ppermute | solution.py:20
  604.6 4.1 collective-permute-start.10
  608.7 2.1 collective-permute-start.11
  610.8 1.3 collective-permute-start.6
  612.1 0.7 pad_clamp_fusion.4
  612.7 0.7 pad_clamp_fusion
  613.4 1.4 fusion.36
  614.8 1.3 collective-permute-start.13
  617.3 0.6 gather_fusion.1
  618.6 0.6 gather_fusion.2
  619.8 0.6 gather_fusion.4
  620.5 0.6 gather_fusion.5
  621.1 0.6 gather_fusion.6
  621.8 0.6 gather_fusion
  622.4 2.7 collective-permute-start.14
  625.1 3.6 collective-permute-done.10
  628.7 1.9 collective-permute-start.15
  630.6 12.4 %collective-permute-done.11 = bf16[4,512,128]{2,1,0:T(8,128)(2,1)} collective-permute-done((bf16[4,512,128]{2,1,0:T(8,128)(2,1)S(1)}, bf16[4,512,128]{2,1,0:T(8,128)(2,1)}, u32[]{:S(2)}, u32[]{:S(2)}) %collective-permute-start.11) | collective-permute-done | bytes 524320 | tf_op jit(solution)/shard_map/ppermute | solution.py:20
  643.1 2.1 collective-permute-start.16
  645.2 6.4 collective-permute-start.17
  651.6 0.7 fusion.55
  652.4 1.3 collective-permute-start.12
  653.7 2.5 gather_fusion.8
  656.2 2.4 gather_fusion.9
  658.7 1.4 gather_fusion.11
  660.1 2.4 gather_fusion.12
  662.6 2.5 gather_fusion.13
  665.1 2.5 gather_fusion.7
  667.5 2.5 gather_fusion.15
  670.0 2.5 gather_fusion.16
  672.5 2.5 gather_fusion.18
  675.0 2.4 gather_fusion.19
  677.5 2.5 gather_fusion.20
  680.0 3.1 fusion.61
  683.2 1.8 gather_fusion.14
  685.0 1.0 fusion.32
  686.0 0.7 fusion.57
  686.7 0.7 fusion.48
  687.4 0.8 dynamic-slice_bitcast_fusion
  688.2 2.3 fusion.8
  690.5 48.1 %all-gather.1 = bf16[64,4,1024]{2,1,0:T(4,128)(2,1)S(1)} all-gather(bf16[1,4,1024]{2,1,0:T(4,128)(2,1)S(1)} %reshape.335), channel_id=1, replica_groups=mesh['beam'=64,'head'=8] {'beam'}, dimensions={0}, use_global_device_ids=true | all-gather | bytes 532480 | tf_op jit(solution)/shard_map/all_gather | solution.py:147
  738.7 0.9 fusion.62
  739.7 32.2 %reduce-scatter.2.cloned.1.call-done = f32[32,128]{1,0:T(8,128)} async-done(((f32[256,128]{1,0:T(8,128)}), f32[32,128]{1,0:T(8,128)}) %reduce-scatter.2.cloned.1.call-update) | async-done | bytes 16400 | tf_op jit(solution)/shard_map/reduce_scatter | solution.py:151
  771.9 1.3 convert_element_type.55
  (92 shorter events, 5.3 us)
Async XLA Ops:
  6.5 85.1 %copy-start = (bf16[16,256,128]{2,1,0:T(8,128)(2,1)S(1)}, bf16[16,256,128]{2,1,0:T(8,128)(2,1)}, u32[]{:S(2)}) copy-start(bf16[16,256,128]{2,1,0:T(8,128)(2,1)} %param.17) | copy-start | bytes 3145732
  6.5 680.9 %all-reduce.4.cloned.1.call-start = ((), (), s32[]{:S(2)}) async-start(), calls=%async_computation.2 | async-start | bytes 2097152
  7.8 584.7 %collective-permute-start.1 = (bf16[4]{0:T(256)(128)(2,1)}, bf16[4]{0:T(256)(128)(2,1)}, u32[]{:S(2)}, u32[]{:S(2)}) collective-permute-start(bf16[4]{0:T(256)(128)(2,1)} %convert_element_type.44), channel_id=1, source_target_pairs={{16,0},{24,8},{32,16},{40,24},{48,32},{56,40},{64,48},{72,56},{80,... | collective-permute-start | bytes 32 | tf_op jit(solution)/shard_map/ppermute | solution.py:20
  9.1 584.7 %collective-permute-start.2 = (bf16[4]{0:T(256)(128)(2,1)}, bf16[4]{0:T(256)(128)(2,1)}, u32[]{:S(2)}, u32[]{:S(2)}) collective-permute-start(bf16[4]{0:T(256)(128)(2,1)} %convert_element_type.44), channel_id=1, source_target_pairs={{8,0},{16,8},{24,16},{32,24},{40,32},{48,40},{56,48},{64,56},{72,6... | collective-permute-start | bytes 32 | tf_op jit(solution)/shard_map/ppermute | solution.py:20
  17.9 577.2 %collective-permute-start.3 = (bf16[4]{0:T(256)(128)(2,1)}, bf16[4]{0:T(256)(128)(2,1)}, u32[]{:S(2)}, u32[]{:S(2)}) collective-permute-start(bf16[4]{0:T(256)(128)(2,1)} %convert_element_type.44), channel_id=1, source_target_pairs={{0,8},{8,16},{16,24},{24,32},{32,40},{40,48},{48,56},{56,64},{64,7... | collective-permute-start | bytes 32 | tf_op jit(solution)/shard_map/ppermute | solution.py:20
  22.1 588.7 %collective-permute-start.7 = (bf16[4,512,128]{2,1,0:T(8,128)(2,1)}, bf16[4,512,128]{2,1,0:T(8,128)(2,1)}, u32[]{:S(2)}, u32[]{:S(2)}) collective-permute-start(bf16[4,512,128]{2,1,0:T(8,128)(2,1)} %param.19), channel_id=1, source_target_pairs={{16,0},{24,8},{32,16},{40,24},{48,32},{56,40},{64,48},{72,56},{80,... | collective-permute-start | bytes 1572872 | tf_op jit(solution)/shard_map/ppermute | solution.py:20
  23.4 591.4 %collective-permute-start.8 = (bf16[4,512,128]{2,1,0:T(8,128)(2,1)}, bf16[4,512,128]{2,1,0:T(8,128)(2,1)}, u32[]{:S(2)}, u32[]{:S(2)}) collective-permute-start(bf16[4,512,128]{2,1,0:T(8,128)(2,1)} %param.19), channel_id=1, source_target_pairs={{8,0},{16,8},{24,16},{32,24},{40,32},{48,40},{56,48},{64,56},{72,6... | collective-permute-start | bytes 1572872 | tf_op jit(solution)/shard_map/ppermute | solution.py:20
  336.5 1.2 copy-start.2
  338.2 1.3 copy-start.11
  338.2 2.0 copy-start.1
  338.3 3.1 copy-start.3
  338.3 4.7 copy-start.4
  339.5 4.2 copy-start.12
  339.5 274.0 %copy-start.7 = (bf16[4,1024]{1,0:T(4,128)(2,1)S(1)}, bf16[4,1024]{1,0:T(4,128)(2,1)}, u32[]{:S(2)}) copy-start(bf16[4,1024]{1,0:T(4,128)(2,1)} %param.14) | copy-start | bytes 24580
  339.5 432.4 %reduce-scatter.2.cloned.1.call-start = ((), (), s32[]{:S(2)}) async-start(), calls=%async_computation.1 | async-start | bytes 147456 | tf_op jit(solution)/shard_map/reduce_scatter | solution.py:151
  340.2 2.7 copy-start.9
  340.2 2.7 copy-start.10
  592.5 3.9 collective-permute-start.4
  593.8 10.7 %collective-permute-start.5 = (bf16[4]{0:T(256)(128)(2,1)}, bf16[4]{0:T(256)(128)(2,1)S(1)}, u32[]{:S(2)}, u32[]{:S(2)}) collective-permute-start(bf16[4]{0:T(256)(128)(2,1)} %convert_element_type.44), channel_id=1, source_target_pairs={{0,24},{8,32},{16,40},{24,48},{32,56},{40,64},{48,72},{56,80},{64,... | collective-permute-start | bytes 32 | tf_op jit(solution)/shard_map/ppermute | solution.py:20
  595.1 13.6 %collective-permute-start = (bf16[4]{0:T(256)(128)(2,1)}, bf16[4]{0:T(256)(128)(2,1)S(1)}, u32[]{:S(2)}, u32[]{:S(2)}) collective-permute-start(bf16[4]{0:T(256)(128)(2,1)} %convert_element_type.44), channel_id=1, source_target_pairs={{24,0},{32,8},{40,16},{48,24},{56,32},{64,40},{72,48},{80,56},{88,... | collective-permute-start | bytes 32 | tf_op jit(solution)/shard_map/ppermute | solution.py:20
  596.4 26.0 %collective-permute-start.9 = (bf16[4,512,128]{2,1,0:T(8,128)(2,1)S(1)}, bf16[4,512,128]{2,1,0:T(8,128)(2,1)S(1)}, u32[]{:S(2)}, u32[]{:S(2)}) collective-permute-start(bf16[4,512,128]{2,1,0:T(8,128)(2,1)S(1)} %copy-done.3), channel_id=1, source_target_pairs={{0,8},{8,16},{16,24},{24,32},{32,40},{40,48},{48,56},{56,64},{64,7... | collective-permute-start | bytes 1572872 | tf_op jit(solution)/shard_map/ppermute | solution.py:20
  604.6 24.2 %collective-permute-start.10 = (bf16[4,512,128]{2,1,0:T(8,128)(2,1)S(1)}, bf16[4,512,128]{2,1,0:T(8,128)(2,1)}, u32[]{:S(2)}, u32[]{:S(2)}) collective-permute-start(bf16[4,512,128]{2,1,0:T(8,128)(2,1)S(1)} %copy-done.3), channel_id=1, source_target_pairs={{0,16},{8,24},{16,32},{24,40},{32,48},{40,56},{48,64},{56,72},{64,... | collective-permute-start | bytes 1572872 | tf_op jit(solution)/shard_map/ppermute | solution.py:20
  608.7 34.4 %collective-permute-start.11 = (bf16[4,512,128]{2,1,0:T(8,128)(2,1)S(1)}, bf16[4,512,128]{2,1,0:T(8,128)(2,1)}, u32[]{:S(2)}, u32[]{:S(2)}) collective-permute-start(bf16[4,512,128]{2,1,0:T(8,128)(2,1)S(1)} %copy-done.3), channel_id=1, source_target_pairs={{0,24},{8,32},{16,40},{24,48},{32,56},{40,64},{48,72},{56,80},{64,... | collective-permute-start | bytes 1572872 | tf_op jit(solution)/shard_map/ppermute | solution.py:20
  610.8 34.4 %collective-permute-start.6 = (bf16[4,512,128]{2,1,0:T(8,128)(2,1)S(1)}, bf16[4,512,128]{2,1,0:T(8,128)(2,1)}, u32[]{:S(2)}, u32[]{:S(2)}) collective-permute-start(bf16[4,512,128]{2,1,0:T(8,128)(2,1)S(1)} %copy-done.3), channel_id=1, source_target_pairs={{24,0},{32,8},{40,16},{48,24},{56,32},{64,40},{72,48},{80,56},{88,... | collective-permute-start | bytes 1572872 | tf_op jit(solution)/shard_map/ppermute | solution.py:20
  614.8 37.6 %collective-permute-start.13 = (bf16[4,512,128]{2,1,0:T(8,128)(2,1)S(1)}, bf16[4,512,128]{2,1,0:T(8,128)(2,1)}, u32[]{:S(2)}, u32[]{:S(2)}) collective-permute-start(bf16[4,512,128]{2,1,0:T(8,128)(2,1)S(1)} %copy-done.4), channel_id=1, source_target_pairs={{16,0},{24,8},{32,16},{40,24},{48,32},{56,40},{64,48},{72,56},{80,... | collective-permute-start | bytes 1572872 | tf_op jit(solution)/shard_map/ppermute | solution.py:20
  616.7 48.3 %copy-start.8 = (s32[1024]{0:T(1024)}, s32[1024]{0:T(1024)S(1)}, u32[]{:S(2)}) copy-start(s32[1024]{0:T(1024)S(1)} %pad_clamp_fusion.6) | copy-start | bytes 12292
  622.4 47.6 %collective-permute-start.14 = (bf16[4,512,128]{2,1,0:T(8,128)(2,1)S(1)}, bf16[4,512,128]{2,1,0:T(8,128)(2,1)}, u32[]{:S(2)}, u32[]{:S(2)}) collective-permute-start(bf16[4,512,128]{2,1,0:T(8,128)(2,1)S(1)} %copy-done.4), channel_id=1, source_target_pairs={{8,0},{16,8},{24,16},{32,24},{40,32},{48,40},{56,48},{64,56},{72,6... | collective-permute-start | bytes 1572872 | tf_op jit(solution)/shard_map/ppermute | solution.py:20
  628.7 43.8 %collective-permute-start.15 = (bf16[4,512,128]{2,1,0:T(8,128)(2,1)S(1)}, bf16[4,512,128]{2,1,0:T(8,128)(2,1)}, u32[]{:S(2)}, u32[]{:S(2)}) collective-permute-start(bf16[4,512,128]{2,1,0:T(8,128)(2,1)S(1)} %copy-done.4), channel_id=1, source_target_pairs={{0,8},{8,16},{16,24},{24,32},{32,40},{40,48},{48,56},{56,64},{64,7... | collective-permute-start | bytes 1572872 | tf_op jit(solution)/shard_map/ppermute | solution.py:20
  643.1 31.9 %collective-permute-start.16 = (bf16[4,512,128]{2,1,0:T(8,128)(2,1)S(1)}, bf16[4,512,128]{2,1,0:T(8,128)(2,1)}, u32[]{:S(2)}, u32[]{:S(2)}) collective-permute-start(bf16[4,512,128]{2,1,0:T(8,128)(2,1)S(1)} %copy-done.4), channel_id=1, source_target_pairs={{0,16},{8,24},{16,32},{24,40},{32,48},{40,56},{48,64},{56,72},{64,... | collective-permute-start | bytes 1572872 | tf_op jit(solution)/shard_map/ppermute | solution.py:20
  645.2 32.3 %collective-permute-start.17 = (bf16[4,512,128]{2,1,0:T(8,128)(2,1)S(1)}, bf16[4,512,128]{2,1,0:T(8,128)(2,1)}, u32[]{:S(2)}, u32[]{:S(2)}) collective-permute-start(bf16[4,512,128]{2,1,0:T(8,128)(2,1)S(1)} %copy-done.4), channel_id=1, source_target_pairs={{0,24},{8,32},{16,40},{24,48},{32,56},{40,64},{48,72},{56,80},{64,... | collective-permute-start | bytes 1572872 | tf_op jit(solution)/shard_map/ppermute | solution.py:20
  652.3 27.6 %copy-start.20 = (pred[4]{0:T(512)(128)(4,1)}, pred[4]{0:T(512)(128)(4,1)S(1)}, u32[]{:S(2)}) copy-start(pred[4]{0:T(512)(128)(4,1)S(1)} %get-tuple-element.30) | copy-start | bytes 16
  652.3 27.6 %copy-start.21 = (pred[4]{0:T(512)(128)(4,1)}, pred[4]{0:T(512)(128)(4,1)S(1)}, u32[]{:S(2)}) copy-start(pred[4]{0:T(512)(128)(4,1)S(1)} %get-tuple-element.31) | copy-start | bytes 16
  652.3 27.6 %copy-start.22 = (pred[4]{0:T(512)(128)(4,1)}, pred[4]{0:T(512)(128)(4,1)S(1)}, u32[]{:S(2)}) copy-start(pred[4]{0:T(512)(128)(4,1)S(1)} %get-tuple-element.32) | copy-start | bytes 16
  652.3 27.6 %copy-start.23 = (pred[4]{0:T(512)(128)(4,1)}, pred[4]{0:T(512)(128)(4,1)S(1)}, u32[]{:S(2)}) copy-start(pred[4]{0:T(512)(128)(4,1)S(1)} %get-tuple-element.33) | copy-start | bytes 16
  652.3 27.6 %copy-start.24 = (pred[4]{0:T(512)(128)(4,1)}, pred[4]{0:T(512)(128)(4,1)S(1)}, u32[]{:S(2)}) copy-start(pred[4]{0:T(512)(128)(4,1)S(1)} %get-tuple-element.34) | copy-start | bytes 16
  652.3 27.6 %copy-start.25 = (pred[4]{0:T(512)(128)(4,1)}, pred[4]{0:T(512)(128)(4,1)S(1)}, u32[]{:S(2)}) copy-start(pred[4]{0:T(512)(128)(4,1)S(1)} %get-tuple-element.35) | copy-start | bytes 16
  652.3 27.6 %copy-start.26 = (pred[4]{0:T(512)(128)(4,1)}, pred[4]{0:T(512)(128)(4,1)S(1)}, u32[]{:S(2)}) copy-start(pred[4]{0:T(512)(128)(4,1)S(1)} %get-tuple-element.36) | copy-start | bytes 16
  652.4 30.8 %collective-permute-start.12 = (bf16[4,512,128]{2,1,0:T(8,128)(2,1)S(1)}, bf16[4,512,128]{2,1,0:T(8,128)(2,1)}, u32[]{:S(2)}, u32[]{:S(2)}) collective-permute-start(bf16[4,512,128]{2,1,0:T(8,128)(2,1)S(1)} %copy-done.4), channel_id=1, source_target_pairs={{24,0},{32,8},{40,16},{48,24},{56,32},{64,40},{72,48},{80,56},{88,... | collective-permute-start | bytes 1572872 | tf_op jit(solution)/shard_map/ppermute | solution.py:20
  670.0 10.0 %copy-start.5 = (bf16[4,512,128]{2,1,0:T(8,128)(2,1)S(1)}, bf16[4,512,128]{2,1,0:T(8,128)(2,1)}, u32[]{:S(2)}) copy-start(bf16[4,512,128]{2,1,0:T(8,128)(2,1)} %gather_fusion.10) | copy-start | bytes 1572868
  670.0 10.0 %copy-start.13 = (pred[4]{0:T(512)(128)(4,1)S(1)}, pred[4]{0:T(512)(128)(4,1)}, u32[]{:S(2)}) copy-start(pred[4]{0:T(512)(128)(4,1)} %get-tuple-element.11) | copy-start | bytes 16
  670.0 10.0 %copy-start.14 = (pred[4]{0:T(512)(128)(4,1)S(1)}, pred[4]{0:T(512)(128)(4,1)}, u32[]{:S(2)}) copy-start(pred[4]{0:T(512)(128)(4,1)} %get-tuple-element.37) | copy-start | bytes 16
  670.0 10.0 %copy-start.15 = (pred[4]{0:T(512)(128)(4,1)S(1)}, pred[4]{0:T(512)(128)(4,1)}, u32[]{:S(2)}) copy-start(pred[4]{0:T(512)(128)(4,1)} %get-tuple-element.39) | copy-start | bytes 16
  670.0 10.0 %copy-start.16 = (pred[4]{0:T(512)(128)(4,1)S(1)}, pred[4]{0:T(512)(128)(4,1)}, u32[]{:S(2)}) copy-start(pred[4]{0:T(512)(128)(4,1)} %get-tuple-element.41) | copy-start | bytes 16
  670.0 10.0 %copy-start.17 = (pred[4]{0:T(512)(128)(4,1)S(1)}, pred[4]{0:T(512)(128)(4,1)}, u32[]{:S(2)}) copy-start(pred[4]{0:T(512)(128)(4,1)} %get-tuple-element.43) | copy-start | bytes 16
  670.0 10.0 %copy-start.18 = (pred[4]{0:T(512)(128)(4,1)S(1)}, pred[4]{0:T(512)(128)(4,1)}, u32[]{:S(2)}) copy-start(pred[4]{0:T(512)(128)(4,1)} %get-tuple-element.45) | copy-start | bytes 16
  670.0 10.0 %copy-start.19 = (pred[4]{0:T(512)(128)(4,1)S(1)}, pred[4]{0:T(512)(128)(4,1)}, u32[]{:S(2)}) copy-start(pred[4]{0:T(512)(128)(4,1)} %get-tuple-element.47) | copy-start | bytes 16
  688.2 50.6 %copy-start.6 = (bf16[1024,128]{1,0:T(8,128)(2,1)S(1)}, bf16[1024,128]{1,0:T(8,128)(2,1)}, u32[]{:S(2)}) copy-start(bf16[1024,128]{1,0:T(8,128)(2,1)} %param.23) | copy-start | bytes 786436
Sparse Core Ops, SparseCore 0:
  339.6 194.2 all-reduce.3
  739.8 32.0 reduce-scatter.1
where the time goes:
time: 786 us; the launch traced here: 780 us
  blocking collectives  603 us (77%)
  starting transfers between devices  52.6 us (7%)
  waiting for transfers between devices  48.4 us (6%)
  local copies, waits for them, and re-layouts  40.1 us (5%)
  between operations  14.6 us (2%)
  other arithmetic  11.5 us (1%)
  matrix products  9.87 us (1%)
    unnamed x1, blocking collectives  246 us
    pmax x1, blocking collectives, per_device(): prompt_max = lax.pmax(local_max, 'beam')  243 us
    all_gather x1, blocking collectives, per_device(): everyone = lax.all_gather(queries, 'beam', axis=0, tiled=True)  65.4 us
    ppermute x18, starting transfers between devices, shifted(): return lax.ppermute(x, axis, pairs)  52.6 us
    all_gather x1, blocking collectives, per_device(): lax.all_gather(attended, 'beam', axis=0, tiled=True)  48.1 us
    reduce_scatter x1, waiting for transfers between devices, per_device(): lax.psum_scatter(products, 'head', scatter_dimension=0, tiled=True)  32.2 us
    ppermute x18, waiting for transfers between devices, shifted(): return lax.ppermute(x, axis, pairs)  16.1 us
  transfers between devices with their start and end apart: 20, of which 3 were waited for; matrix products, arithmetic and copies ran while one was open for 7% of the time, Pallas kernels for 0%

commit v1 on v0

v1 whole, which is shorter than its diff:
```python
import functools
import math

import jax
import jax.numpy as jnp
from jax import lax
from jax.experimental import pallas as pl
from jax.experimental.pallas import tpu as pltpu
from jax.sharding import PartitionSpec as P

MESH = pl.DeviceIdType.MESH
HD = 128
QPK = 8
OWN_BEAMS = 4
BLOCK_LEN = 128
PRIV = 512
NX, NZ, NY = 4, 8, 8
CHIPS = NX * NZ
SET = 8
SLOTS = CHIPS + 4
TO_LOG2 = 1.0 / math.sqrt(HD) / math.log(2.0)
LOWEST = -3.0e38
LAST = (((1,), (1,)), ((), ()))


def kernel(
    queries, new_keys, new_values, prompt_keys, prompt_values, private_keys, private_values, parents, counts, weight,
    out_ref,
    q_in, nk_in, nv_in, par_in, cnt_in, q_rows, q_mine, q_set, q_own, par_mine, par_all,
    keys, values, values_t, pkeys, pvalues, pvalues_t, self_rows, pscores, w_both,
    num_out, stat_out, num_in, stat_in, att_mine, att_all, part, part_in,
    small_sem, kv_sem, priv_sem, w_sem, pair_send, pair_recv,
    q_send, q_recv, own_send, own_recv, par_send, par_recv,
    num_send, num_recv, stat_send, stat_recv, att_send, att_recv, part_send, part_recv,
):
    d = lax.axis_index("beam")
    y = lax.axis_index("head")
    core = d % 2
    chip = d // 2
    x = chip // NZ
    z = chip % NZ
    request = chip // 2
    home = request // SET
    slot = request % SET
    member = d % 4

    barrier = pltpu.get_barrier_semaphore()

    def greet_plane(k, carry):
        pl.semaphore_signal(barrier, inc=1, device_id=((d + k) % 64, y), device_id_type=MESH)
        return carry

    def greet_column(k, carry):
        pl.semaphore_signal(barrier, inc=1, device_id=(chip * 2 + k % 2, (y + 1 + k // 2) % NY), device_id_type=MESH)
        return carry

    lax.fori_loop(1, 64, greet_plane, 0)
    lax.fori_loop(0, 14, greet_column, 0)

    small = [
        pltpu.make_async_copy(src, dst, small_sem.at[n])
        for n, (src, dst) in enumerate(
            ((queries, q_in), (new_keys, nk_in), (new_values, nv_in), (parents, par_in), (counts, cnt_in))
        )
    ]
    for copy in small:
        copy.start()
    private = [
        pltpu.make_async_copy(private_keys, pkeys, priv_sem.at[0]),
        pltpu.make_async_copy(private_values, pvalues, priv_sem.at[1]),
    ]
    for copy in private:
        copy.start()
    mine = pl.ds(core * SET, SET)
    theirs = pl.ds((1 - core) * SET, SET)
    cached = [
        pltpu.make_async_copy(prompt_keys.at[mine], keys.at[:, 0], kv_sem.at[0]),
        pltpu.make_async_copy(prompt_values.at[mine], values.at[:, 0], kv_sem.at[1]),
    ]
    for copy in cached:
        copy.start()
    own_weight = pltpu.make_async_copy(weight, w_both.at[core], w_sem.at[0])
    own_weight.start()
    pair = (chip * 2 + 1 - core, y)
    swaps = [
        pltpu.make_async_remote_copy(
            src, dst, pair_send.at[n], pair_recv.at[n], device_id=pair, device_id_type=MESH
        )
        for n, (src, dst) in enumerate(
            (
                (prompt_keys.at[theirs], keys.at[:, 1]),
                (prompt_values.at[theirs], values.at[:, 1]),
                (weight, w_both.at[core]),
            )
        )
    ]

    small[0].wait()
    q_wide = q_in[...].astype(jnp.float32)
    for head in range(QPK):
        q_rows[pl.ds(head * OWN_BEAMS, OWN_BEAMS), :] = q_wide[:, head * HD : (head + 1) * HD]
    q_mine[...] = q_rows[...].astype(jnp.bfloat16)
    lane = lax.broadcasted_iota(jnp.int32, (8, HD), 1)
    small[3].wait()
    row_parent = jnp.zeros((8, HD), jnp.int32)
    for beam in range(OWN_BEAMS):
        row_parent = jnp.where(lane % OWN_BEAMS == beam, par_in[beam], row_parent)
    par_mine[...] = jnp.where(lane // 32 == member, row_parent, 0)

    pl.semaphore_wait(barrier, 77)

    def own_copy(j):
        to = (request * 4 + j, y)
        return (
            pltpu.make_async_remote_copy(
                q_mine, q_own.at[member], own_send.at[j], own_recv.at[0], device_id=to, device_id_type=MESH
            ),
            pltpu.make_async_remote_copy(
                par_mine, par_all.at[member], par_send.at[j], par_recv.at[0], device_id=to, device_id_type=MESH
            ),
        )

    def own_start(j, carry):
        @pl.when(j != member)
        def _():
            for copy in own_copy(j):
                copy.start()

        return carry

    def own_done(j, carry):
        @pl.when(j != member)
        def _():
            for copy in own_copy(j):
                copy.wait_send()

        return carry

    lax.fori_loop(0, 4, own_start, 0)
    pltpu.make_async_copy(q_mine, q_own.at[member], own_recv.at[0]).start()
    pltpu.make_async_copy(par_mine, par_all.at[member], par_recv.at[0]).start()

    def q_target(n):
        return (4 * ((slot - n // 4 + 8) % 8) + (chip + n) % 4) * 2 + home

    def q_copy(n):
        return pltpu.make_async_remote_copy(
            q_mine, q_set.at[slot, member], q_send.at[n], q_recv.at[slot], device_id=(q_target(n), y), device_id_type=MESH
        )

    def q_start(n, carry):
        @pl.when(q_target(n) != d)
        def _():
            q_copy(n).start()

        return carry

    def q_done(n, carry):
        @pl.when(q_target(n) != d)
        def _():
            q_copy(n).wait_send()

        return carry

    lax.fori_loop(0, CHIPS, q_start, 0)

    @pl.when(home == core)
    def _():
        pltpu.make_async_copy(q_mine, q_set.at[slot, member], q_recv.at[slot]).start()

    for copy in swaps:
        copy.start()

    private[1].wait()

    def turn_private(j, carry):
        pvalues_t[j] = pvalues[j].T
        return carry

    lax.fori_loop(0, OWN_BEAMS, turn_private, 0)
    small[1].wait()
    small[2].wait()
    small[4].wait()
    self_rows[...] = jnp.zeros_like(self_rows)
    self_rows[0, pl.ds(0, OWN_BEAMS), :] = nk_in[...].astype(jnp.float32)
    self_rows[1, pl.ds(0, OWN_BEAMS), :] = nv_in[...].astype(jnp.float32)
    self_keys = self_rows[0].astype(jnp.bfloat16)
    self_values_t = self_rows[1].T.astype(jnp.bfloat16)

    private[0].wait()
    pltpu.make_async_copy(q_own, q_own, own_recv.at[0]).wait()
    pltpu.make_async_copy(par_all, par_all, par_recv.at[0]).wait()
    q_request = q_own[...].reshape(128, HD)
    row_parent = par_all[0] + par_all[1] + par_all[2] + par_all[3]
    row_parent = row_parent[0:1, :]
    position = lax.broadcasted_iota(jnp.int32, (PRIV, HD), 0)
    at = lax.broadcasted_iota(jnp.int32, (HD, HD), 0)
    across = lax.broadcasted_iota(jnp.int32, (HD, HD), 1)
    scores = lax.dot_general(self_keys, q_request, LAST, preferred_element_type=jnp.float32) * TO_LOG2
    is_own = jnp.logical_and(across // 32 == member, across % OWN_BEAMS == at)
    self_scores = jnp.where(is_own, scores, LOWEST)

    def private_scores(j, highest):
        got = lax.dot_general(pkeys[j], q_request, LAST, preferred_element_type=jnp.float32) * TO_LOG2
        filled = jnp.where(row_parent == d * OWN_BEAMS + j, cnt_in[j] * BLOCK_LEN, 0)
        got = jnp.where(position < filled, got, LOWEST)
        pscores[j] = got
        return jnp.maximum(highest, jnp.max(got, axis=0, keepdims=True))

    highest = lax.fori_loop(0, OWN_BEAMS, private_scores, jnp.max(self_scores, axis=0, keepdims=True))
    weights = jnp.where(self_scores > LOWEST, jnp.exp2(self_scores - highest), 0.0)
    total = jnp.sum(weights, axis=0, keepdims=True)
    summed = jnp.dot(self_values_t, weights.astype(jnp.bfloat16), preferred_element_type=jnp.float32)

    def private_sums(j, carry):
        total, summed = carry
        got = pscores[j]
        weights = jnp.where(got > LOWEST, jnp.exp2(got - highest), 0.0)
        total = total + jnp.sum(weights, axis=0, keepdims=True)
        summed = summed + jnp.dot(pvalues_t[j], weights.astype(jnp.bfloat16), preferred_element_type=jnp.float32)
        return total, summed

    total, summed = lax.fori_loop(0, OWN_BEAMS, private_sums, (total, summed))
    num_out[SET] = summed.astype(jnp.bfloat16)
    stat_out[SET, 0:1, :] = highest
    stat_out[SET, 1:2, :] = total

    def result_copies(source, owner_slot, to_core, into, n, quarter):
        owner = 4 * owner_slot + quarter
        rows = pl.ds(pl.multiple_of(quarter * 32, 32), 32)
        to = (owner * 2 + to_core, y)
        return (
            to[0] != d,
            (
                pltpu.make_async_remote_copy(
                    num_out.at[source, rows], num_in.at[into], num_send.at[n], num_recv.at[0],
                    device_id=to, device_id_type=MESH,
                ),
                pltpu.make_async_remote_copy(
                    stat_out.at[source], stat_in.at[into], stat_send.at[n], stat_recv.at[0],
                    device_id=to, device_id_type=MESH,
                ),
            ),
            (
                pltpu.make_async_copy(num_out.at[source, rows], num_in.at[into], num_recv.at[0]),
                pltpu.make_async_copy(stat_out.at[source], stat_in.at[into], stat_recv.at[0]),
            ),
        )

    def prompt_result(n):
        owner_slot = (chip // 4 + n // 4) % SET
        return result_copies(owner_slot, owner_slot, core, chip, n, (chip + n) % 4)

    def private_result(j):
        return result_copies(SET, slot, home, CHIPS + member, CHIPS + j, (chip + j) % 4)

    def result_start(make, n):
        remote, far, near = make(n)

        @pl.when(remote)
        def _():
            for copy in far:
                copy.start()

        @pl.when(jnp.logical_not(remote))
        def _():
            for copy in near:
                copy.start()

    def result_done(make, n):
        remote, far, _ = make(n)

        @pl.when(remote)
        def _():
            for copy in far:
                copy.wait_send()

    def private_start(j, carry):
        result_start(private_result, j)
        return carry

    lax.fori_loop(0, 4, private_start, 0)

    for copy in cached:
        copy.wait()
    for copy in swaps[:2]:
        copy.wait_recv()

    def turn(i, carry):
        values_t[i] = values[i].reshape(512, HD).T
        return carry

    lax.fori_loop(0, SET, turn, 0)

    def one_request(s, carry):
        i = (chip // 4 + s) % SET
        pltpu.make_async_copy(q_set.at[i], q_set.at[i], q_recv.at[i]).wait()
        rows = q_set[i].reshape(128, HD)
        scores = (
            lax.dot_general(keys[i].reshape(512, HD), rows, LAST, preferred_element_type=jnp.float32) * TO_LOG2
        )
        highest = jnp.max(scores, axis=0, keepdims=True)
        weights = jnp.exp2(scores - highest)
        stat_out[i, 0:1, :] = highest
        stat_out[i, 1:2, :] = jnp.sum(weights, axis=0, keepdims=True)
        num_out[i] = jnp.dot(
            values_t[i], weights.astype(jnp.bfloat16), preferred_element_type=jnp.float32
        ).astype(jnp.bfloat16)
        for j in range(4):
            result_start(prompt_result, s * 4 + j)
        return carry

    lax.fori_loop(0, SET, one_request, 0)

    lax.fori_loop(0, 4, own_done, 0)
    lax.fori_loop(0, CHIPS, q_done, 0)
    for copy in swaps:
        copy.wait_send()

    pltpu.make_async_copy(stat_in, stat_in, stat_recv.at[0]).wait()
    stats = [stat_in[k] for k in range(SLOTS)]
    highest = stats[0][0:1, :]
    for k in range(1, SLOTS):
        highest = jnp.maximum(highest, stats[k][0:1, :])
    shares = [jnp.exp2(stats[k][0:1, :] - highest) for k in range(SLOTS)]
    total = shares[0] * stats[0][1:2, :]
    for k in range(1, SLOTS):
        total = total + shares[k] * stats[k][1:2, :]
    pltpu.make_async_copy(num_in, num_in, num_recv.at[0]).wait()
    summed = shares[0] * num_in[0].astype(jnp.float32)
    for k in range(1, SLOTS):
        summed = summed + shares[k] * num_in[k].astype(jnp.float32)
    attended = (summed / total).astype(jnp.bfloat16).astype(jnp.float32)

    head_of = lax.broadcasted_iota(jnp.int32, (32, HD), 1) // OWN_BEAMS % QPK
    spread = jnp.concatenate(
        [jnp.where(head_of == head, attended, 0.0).astype(jnp.bfloat16) for head in range(QPK)], axis=0
    )
    beam_at = lax.broadcasted_iota(jnp.int32, (16, HD), 0)
    beam_lane = lax.broadcasted_iota(jnp.int32, (16, HD), 1)
    chosen = (beam_lane // 32 * OWN_BEAMS + beam_lane % OWN_BEAMS == beam_at).astype(jnp.float32)
    att_mine[...] = lax.dot_general(
        chosen.astype(jnp.bfloat16), spread, LAST, preferred_element_type=jnp.float32
    ).astype(jnp.bfloat16)

    place = att_all.at[chip % 4, chip // 4]

    def att_copy(k):
        to = ((((x + k // NZ) % NX) * NZ + (z + k) % NZ) * 2 + core, y)
        return pltpu.make_async_remote_copy(
            att_mine, place, att_send.at[k], att_recv.at[0], device_id=to, device_id_type=MESH
        )

    def att_start(k, carry):
        att_copy(k).start()
        return carry

    def att_done(k, carry):
        att_copy(k).wait_send()
        return carry

    lax.fori_loop(1, CHIPS, att_start, 0)
    pltpu.make_async_copy(att_mine, place, att_recv.at[0]).start()

    def prompt_done(n, carry):
        result_done(prompt_result, n)
        return carry

    def private_done(n, carry):
        result_done(private_result, n)
        return carry

    lax.fori_loop(0, CHIPS, prompt_done, 0)
    lax.fori_loop(0, 4, private_done, 0)
    own_weight.wait()
    swaps[2].wait_recv()

    pltpu.make_async_copy(att_all, att_all, att_recv.at[0]).wait()
    rows = [att_all[quarter].reshape(128, 256) for quarter in range(4)]
    for side in range(2):
        product = jnp.zeros((128, HD), jnp.float32)
        for quarter in range(4):
            product = product + jnp.dot(
                rows[quarter], w_both[side, :, quarter].reshape(256, HD), preferred_element_type=jnp.float32
            )
        part[side] = product.astype(jnp.bfloat16).reshape(4, 32, HD)

    def part_target(n):
        return chip * 2 + n % 2, core * 4 + (y + n // 2) % 4

    def part_copy(n):
        to = part_target(n)
        return pltpu.make_async_remote_copy(
            part.at[n % 2, (y + n // 2) % 4], part_in.at[y], part_send.at[n], part_recv.at[0],
            device_id=to, device_id_type=MESH,
        )

    def part_is_far(n):
        to = part_target(n)
        return jnp.logical_or(to[0] != d, to[1] != y)

    def part_start(n, carry):
        @pl.when(part_is_far(n))
        def _():
            part_copy(n).start()

        return carry

    def part_done(n, carry):
        @pl.when(part_is_far(n))
        def _():
            part_copy(n).wait_send()

        return carry

    lax.fori_loop(0, 8, part_start, 0)

    @pl.when(y // 4 == core)
    def _():
        pltpu.make_async_copy(part.at[core, y % 4], part_in.at[y], part_recv.at[0]).start()

    lax.fori_loop(1, CHIPS, att_done, 0)
    pltpu.make_async_copy(part_in, part_in, part_recv.at[0]).wait()
    mixed = part_in[0].astype(jnp.float32)
    for k in range(1, NY):
        mixed = mixed + part_in[k].astype(jnp.float32)
    out_ref[...] = mixed.astype(jnp.bfloat16)
    lax.fori_loop(0, 8, part_done, 0)


def per_device(
    queries, new_keys, new_values, prompt_keys, prompt_values, private_keys, private_values, parents, counts, weight
):
    bf16, f32, i32 = jnp.bfloat16, jnp.float32, jnp.int32
    dma = pltpu.SemaphoreType.DMA
    anywhere = pl.BlockSpec(memory_space=pl.ANY)
    return pl.pallas_call(
        kernel,
        out_shape=jax.ShapeDtypeStruct((32, HD), bf16),
        in_specs=[anywhere] * 10,
        out_specs=pl.BlockSpec(memory_space=pltpu.VMEM),
        scratch_shapes=[
            pltpu.VMEM((OWN_BEAMS, QPK * HD), bf16),
            pltpu.VMEM((OWN_BEAMS, HD), bf16),
            pltpu.VMEM((OWN_BEAMS, HD), bf16),
            pltpu.SMEM((OWN_BEAMS,), i32),
            pltpu.SMEM((OWN_BEAMS,), i32),
            pltpu.VMEM((32, HD), f32),
            pltpu.VMEM((32, HD), bf16),
            pltpu.VMEM((SET, 4, 32, HD), bf16),
            pltpu.VMEM((4, 32, HD), bf16),
            pltpu.VMEM((8, HD), i32),
            pltpu.VMEM((4, 8, HD), i32),
            pltpu.VMEM((SET, 2, 256, HD), bf16),
            pltpu.VMEM((SET, 2, 256, HD), bf16),
            pltpu.VMEM((SET, HD, 512), bf16),
            pltpu.VMEM((OWN_BEAMS, PRIV, HD), bf16),
            pltpu.VMEM((OWN_BEAMS, PRIV, HD), bf16),
            pltpu.VMEM((OWN_BEAMS, HD, PRIV), bf16),
            pltpu.VMEM((2, HD, HD), f32),
            pltpu.VMEM((OWN_BEAMS, PRIV, HD), f32),
            pltpu.VMEM((2, QPK, 4, 32, HD), bf16),
            pltpu.VMEM((SET + 1, HD, HD), bf16),
            pltpu.VMEM((SET + 1, 2, HD), f32),
            pltpu.VMEM((SLOTS, 32, HD), bf16),
            pltpu.VMEM((SLOTS, 2, HD), f32),
            pltpu.VMEM((16, 256), bf16),
            pltpu.VMEM((4, SET, 16, 256), bf16),
            pltpu.VMEM((2, 4, 32, HD), bf16),
            pltpu.VMEM((NY, 32, HD), bf16),
            dma((5,)), dma((2,)), dma((2,)), dma((1,)), dma((3,)), dma((3,)),
            dma((CHIPS,)), dma((SET,)), dma((4,)), dma((1,)), dma((4,)), dma((1,)),
            dma((SLOTS,)), dma((1,)), dma((SLOTS,)), dma((1,)), dma((CHIPS,)), dma((1,)), dma((8,)), dma((1,)),
        ],
        compiler_params=pltpu.CompilerParams(
            collective_id=0, has_side_effects=True, vmem_limit_bytes=48 << 20
        ),
    )(
        queries, new_keys, new_values, prompt_keys, prompt_values, private_keys, private_values, parents, counts,
        weight.reshape(QPK, 4, 32, HD),
    )


def solution(mesh):
    placed = (
        P("beam", "head"),
        P("beam", "head"),
        P("beam", "head"),
        P(None, "beam", "head"),
        P(None, "beam", "head"),
        P("beam", None, "head"),
        P("beam", None, "head"),
        P("beam"),
        P("beam"),
        P("head", "beam"),
    )
    return jax.shard_map(per_device, mesh=mesh, in_specs=placed, out_specs=P("head", "beam"), check_vma=False)
```

time: 786 us -> 60.8 us (0.08)
  blocking collectives: 603 us -> 0 us
  starting transfers between devices: 52.6 us -> 0 us
  Pallas kernels: 0 us -> 51.5 us
  waiting for transfers between devices: 48.4 us -> 0 us
  local copies, waits for them, and re-layouts: 40.1 us -> 8.8 us
  between operations: 14.6 us -> 0.02 us
  other arithmetic: 11.5 us -> 0 us
  matrix products: 9.87 us -> 0 us
    unnamed x1 -> x0, blocking collectives: 246 us -> none
    pmax x1 -> x0, blocking collectives: 243 us -> none  [per_device(): prompt_max = lax.pmax(local_max, 'beam')]
    all_gather x2 -> x0, blocking collectives: 113 us -> none  [the longest x1 65.4 us: per_device(): everyone = lax.all_gather(queries, 'beam', axis=0, tiled=True)]
    ppermute x18 -> x0, starting transfers between devices: 52.6 us -> none  [shifted(): return lax.ppermute(x, axis, pairs)]
    pallas_call x0 -> x1, Pallas kernels: none -> 51.5 us  [per_device(): pl.pallas_call(kernel, out_shape=jax.ShapeDtypeStruct((32, HD), bf16), in...]
    gather x21 -> x0, local copies, waits for them, and re-layouts: 34.9 us -> none  [the longest x7 15.2 us: per_device(): jnp.take(source[0], picked_rows, axis=0)]
    reduce_scatter x1 -> x0, waiting for transfers between devices: 32.2 us -> none  [per_device(): lax.psum_scatter(products, 'head', scatter_dimension=0, tiled=True)]
    ppermute x18 -> x0, waiting for transfers between devices: 16.1 us -> none  [shifted(): return lax.ppermute(x, axis, pairs)]
  transfers between devices with their start and end apart: 20 -> 0, of which waited for: 3 -> 0; matrix products, arithmetic and copies ran while one was open for 7% -> 0% of each run, Pallas kernels for 0% -> 0%
where the time goes in v1:
time: 60.8 us; the launch traced here: 60.4 us
  Pallas kernels  51.5 us (85%)
  local copies, waits for them, and re-layouts  8.8 us (14%)
    pallas_call x1, Pallas kernels, per_device(): pl.pallas_call(kernel, out_shape=jax.ShapeDtypeStruct((32, HD), bf16), in...  51.5 us
    unnamed x21, local copies, waits for them, and re-layouts  8.8 us

profile of v1, /device:TPU:1, one launch (start us, length us, event | category | flops | bytes accessed | tf_op | source)
XLA Modules:
  0.0 60.4 jit_solution(3350002996797281025)
XLA Ops:
  0.0 0.0 copy-start.8
  0.0 0.0 copy-start.6
  0.0 0.7 %copy-done.8 = s32[4]{0:T(128)S(1)} copy-done((s32[4]{0:T(128)S(1)}, s32[4]{0:T(128)}, u32[]{:S(2)}) %copy-start.8) | copy-done | bytes 40
  0.7 0.0 copy-done.6
  0.7 0.0 copy-start
  0.7 1.2 %copy-done = bf16[16,256,128]{2,1,0:T(8,128)(2,1)S(1)} copy-done((bf16[16,256,128]{2,1,0:T(8,128)(2,1)S(1)}, bf16[16,256,128]{2,1,0:T(8,128)(2,1)}, u32[]{:S(2)}) %copy-start) | copy-done | bytes 1048600
  1.9 0.0 copy-start.1
  1.9 1.2 %copy-done.1 = bf16[16,256,128]{2,1,0:T(8,128)(2,1)S(1)} copy-done((bf16[16,256,128]{2,1,0:T(8,128)(2,1)S(1)}, bf16[16,256,128]{2,1,0:T(8,128)(2,1)}, u32[]{:S(2)}) %copy-start.1) | copy-done | bytes 1048600
  3.1 0.0 copy-start.2
  3.1 1.0 %copy-done.2 = bf16[4,512,128]{2,1,0:T(8,128)(2,1)S(1)} copy-done((bf16[4,512,128]{2,1,0:T(8,128)(2,1)S(1)}, bf16[4,512,128]{2,1,0:T(8,128)(2,1)}, u32[]{:S(2)}) %copy-start.2) | copy-done | bytes 524312
  4.2 0.0 copy-start.3
  4.2 1.0 %copy-done.3 = bf16[4,512,128]{2,1,0:T(8,128)(2,1)S(1)} copy-done((bf16[4,512,128]{2,1,0:T(8,128)(2,1)S(1)}, bf16[4,512,128]{2,1,0:T(8,128)(2,1)}, u32[]{:S(2)}) %copy-start.3) | copy-done | bytes 524312
  5.2 0.0 copy-start.4
  5.2 0.9 %copy-done.4 = bf16[1024,128]{1,0:T(8,128)(2,1)S(1)} copy-done((bf16[1024,128]{1,0:T(8,128)(2,1)S(1)}, bf16[1024,128]{1,0:T(8,128)(2,1)}, u32[]{:S(2)}) %copy-start.4) | copy-done | bytes 262168
  6.2 0.0 copy-start.5
  6.2 0.7 %copy-done.5 = bf16[4,1024]{1,0:T(4,128)(2,1)S(1)} copy-done((bf16[4,1024]{1,0:T(4,128)(2,1)S(1)}, bf16[4,1024]{1,0:T(4,128)(2,1)}, u32[]{:S(2)}) %copy-start.5) | copy-done | bytes 8216
  6.9 0.0 copy-start.7
  6.9 0.7 %copy-done.7 = bf16[4,128]{1,0:T(4,128)(2,1)S(1)} copy-done((bf16[4,128]{1,0:T(4,128)(2,1)S(1)}, bf16[4,128]{1,0:T(4,128)(2,1)}, u32[]{:S(2)}) %copy-start.7) | copy-done | bytes 1048
  7.6 0.0 copy-start.9
  7.6 0.7 %copy-done.9 = s32[4]{0:T(128)S(1)} copy-done((s32[4]{0:T(128)S(1)}, s32[4]{0:T(128)}, u32[]{:S(2)}) %copy-start.9) | copy-done | bytes 40
  8.2 51.5 %shard_map.100 = bf16[32,128]{1,0:T(8,128)(2,1)S(1)} custom-call(bf16[4,1024]{1,0:T(4,128)(2,1)S(1)} %copy-done.5, bf16[4,128]{1,0:T(4,128)(2,1)S(1)} %copy-done.6, bf16[4,128]{1,0:T(4,128)(2,1)S(1)} %copy-done.7, bf16[16,256,128]{2,1,0:T(8,128)(2,1)S(1)} %copy-done, bf16[16,256,128]{2,1,0:T(8,128)(2,1)S(1)} %copy-done.1, ...), custom_call_target="tpu_custom_call" | custom-call | tf_op jit(solution)/shard_map/pallas_call | solution.py:437
  59.7 0.6 copy.12
Async XLA Ops:
  0.0 0.7 %copy-start.8 = (s32[4]{0:T(128)S(1)}, s32[4]{0:T(128)}, u32[]{:S(2)}) copy-start(s32[4]{0:T(128)} %parents.1) | copy-start | bytes 52
  0.0 0.7 %copy-start.6 = (bf16[4,128]{1,0:T(4,128)(2,1)S(1)}, bf16[4,128]{1,0:T(4,128)(2,1)}, u32[]{:S(2)}) copy-start(bf16[4,128]{1,0:T(4,128)(2,1)} %new_keys.1) | copy-start | bytes 3076
  0.7 1.2 %copy-start = (bf16[16,256,128]{2,1,0:T(8,128)(2,1)S(1)}, bf16[16,256,128]{2,1,0:T(8,128)(2,1)}, u32[]{:S(2)}) copy-start(bf16[16,256,128]{2,1,0:T(8,128)(2,1)} %prompt_keys.1) | copy-start | bytes 3145732
  1.9 1.2 %copy-start.1 = (bf16[16,256,128]{2,1,0:T(8,128)(2,1)S(1)}, bf16[16,256,128]{2,1,0:T(8,128)(2,1)}, u32[]{:S(2)}) copy-start(bf16[16,256,128]{2,1,0:T(8,128)(2,1)} %prompt_values.1) | copy-start | bytes 3145732
  3.1 1.0 %copy-start.2 = (bf16[4,512,128]{2,1,0:T(8,128)(2,1)S(1)}, bf16[4,512,128]{2,1,0:T(8,128)(2,1)}, u32[]{:S(2)}) copy-start(bf16[4,512,128]{2,1,0:T(8,128)(2,1)} %private_keys.1) | copy-start | bytes 1572868
  4.2 1.0 %copy-start.3 = (bf16[4,512,128]{2,1,0:T(8,128)(2,1)S(1)}, bf16[4,512,128]{2,1,0:T(8,128)(2,1)}, u32[]{:S(2)}) copy-start(bf16[4,512,128]{2,1,0:T(8,128)(2,1)} %private_values.1) | copy-start | bytes 1572868
  5.2 0.9 %copy-start.4 = (bf16[1024,128]{1,0:T(8,128)(2,1)S(1)}, bf16[1024,128]{1,0:T(8,128)(2,1)}, u32[]{:S(2)}) copy-start(bf16[1024,128]{1,0:T(8,128)(2,1)} %param.19) | copy-start | bytes 786436
  6.2 0.7 %copy-start.5 = (bf16[4,1024]{1,0:T(4,128)(2,1)S(1)}, bf16[4,1024]{1,0:T(4,128)(2,1)}, u32[]{:S(2)}) copy-start(bf16[4,1024]{1,0:T(4,128)(2,1)} %queries.1) | copy-start | bytes 24580
  6.9 0.7 %copy-start.7 = (bf16[4,128]{1,0:T(4,128)(2,1)S(1)}, bf16[4,128]{1,0:T(4,128)(2,1)}, u32[]{:S(2)}) copy-start(bf16[4,128]{1,0:T(4,128)(2,1)} %new_values.1) | copy-start | bytes 3076
  7.6 0.7 %copy-start.9 = (s32[4]{0:T(128)S(1)}, s32[4]{0:T(128)}, u32[]{:S(2)}) copy-start(s32[4]{0:T(128)} %counts.1) | copy-start | bytes 52

commit v2 on v1

--- a/solution.py
+++ b/solution.py
@@ -1,4 +1,3 @@
-import functools
 import math
 
 import jax
@@ -44,18 +43,13 @@
     slot = request % SET
     member = d % 4
 
-    barrier = pltpu.get_barrier_semaphore()
-
-    def greet_plane(k, carry):
-        pl.semaphore_signal(barrier, inc=1, device_id=((d + k) % 64, y), device_id_type=MESH)
-        return carry
-
-    def greet_column(k, carry):
-        pl.semaphore_signal(barrier, inc=1, device_id=(chip * 2 + k % 2, (y + 1 + k // 2) % NY), device_id_type=MESH)
-        return carry
-
-    lax.fori_loop(1, 64, greet_plane, 0)
-    lax.fori_loop(0, 14, greet_column, 0)
+    def far_first(k):
+        u, t = k % NX, k // NX
+        return (2 + (u + 1) // 2 * (1 - 2 * (u % 2))) % NX, (4 + (t + 1) // 2 * (1 - 2 * (t % 2))) % NZ
+
+    def same_core(k):
+        dx, dz = far_first(k)
+        return (((x + dx) % NX) * NZ + (z + dz) % NZ) * 2 + core, y
 
     small = [
         pltpu.make_async_copy(src, dst, small_sem.at[n])
@@ -65,6 +59,38 @@
     ]
     for copy in small:
         copy.start()
+    barrier = pltpu.get_barrier_semaphore()
+
+    def tell(to):
+        pl.semaphore_signal(barrier, inc=1, device_id=to, device_id_type=MESH)
+
+    def tell_same(k, carry):
+        tell(same_core(k))
+        return carry
+
+    def tell_other(k, carry):
+        tell(((core * 16 + (chip + 8 + k) % 16) * 2 + 1 - core, y))
+        return carry
+
+    def tell_column(k, carry):
+        to = (y + 4 + k) % NY
+        row = chip * 2 + y // 4
+
+        @pl.when(jnp.logical_or(row != d, to != y))
+        def _():
+            tell((row, to))
+
+        return carry
+
+    lax.fori_loop(0, CHIPS - 1, tell_same, 0, unroll=True)
+    lax.fori_loop(0, 16, tell_other, 0, unroll=True)
+    lax.fori_loop(0, NY, tell_column, 0, unroll=True)
+
+    @pl.when(home != core)
+    def _():
+        tell((chip * 2 + 1 - core, y))
+        tell(((chip + 1 - 2 * (chip % 2)) * 2 + 1 - core, y))
+
     private = [
         pltpu.make_async_copy(private_keys, pkeys, priv_sem.at[0]),
         pltpu.make_async_copy(private_values, pvalues, priv_sem.at[1]),
@@ -107,16 +133,16 @@
         row_parent = jnp.where(lane % OWN_BEAMS == beam, par_in[beam], row_parent)
     par_mine[...] = jnp.where(lane // 32 == member, row_parent, 0)
 
-    pl.semaphore_wait(barrier, 77)
+    pl.semaphore_wait(barrier, jnp.where(home == core, 33, 63) + jnp.where(y // 4 == core, 7, 8))
 
     def own_copy(j):
         to = (request * 4 + j, y)
         return (
             pltpu.make_async_remote_copy(
-                q_mine, q_own.at[member], own_send.at[j], own_recv.at[0], device_id=to, device_id_type=MESH
+                q_mine, q_own.at[member], own_send.at[0], own_recv.at[0], device_id=to, device_id_type=MESH
             ),
             pltpu.make_async_remote_copy(
-                par_mine, par_all.at[member], par_send.at[j], par_recv.at[0], device_id=to, device_id_type=MESH
+                par_mine, par_all.at[member], par_send.at[0], par_recv.at[0], device_id=to, device_id_type=MESH
             ),
         )
 
@@ -128,24 +154,34 @@
 
         return carry
 
-    def own_done(j, carry):
-        @pl.when(j != member)
-        def _():
-            for copy in own_copy(j):
-                copy.wait_send()
-
-        return carry
-
-    lax.fori_loop(0, 4, own_start, 0)
+    def sent(blocks, sem, count):
+        pltpu.make_async_copy(blocks.at[pl.ds(0, count)], blocks.at[pl.ds(0, count)], sem.at[0]).wait()
+
+    def sent_either(blocks, sem, fewer, count):
+        @pl.when(fewer)
+        def _():
+            sent(blocks, sem, count - 1)
+
+        @pl.when(jnp.logical_not(fewer))
+        def _():
+            sent(blocks, sem, count)
+
+    lax.fori_loop(0, 4, own_start, 0, unroll=True)
     pltpu.make_async_copy(q_mine, q_own.at[member], own_recv.at[0]).start()
     pltpu.make_async_copy(par_mine, par_all.at[member], par_recv.at[0]).start()
 
+    def turn_x(s):
+        u = s // 2
+        return (2 + (u + 1) // 2 * (1 - 2 * (u % 2))) % NX
+
     def q_target(n):
-        return (4 * ((slot - n // 4 + 8) % 8) + (chip + n) % 4) * 2 + home
+        to_x = (slot // 2 - turn_x(n // 4) + NX) % NX
+        to_z = 4 * ((slot + 1 + n // 4) % 2) + (z + n) % 4
+        return (to_x * NZ + to_z) * 2 + home
 
     def q_copy(n):
         return pltpu.make_async_remote_copy(
-            q_mine, q_set.at[slot, member], q_send.at[n], q_recv.at[slot], device_id=(q_target(n), y), device_id_type=MESH
+            q_mine, q_set.at[slot, member], q_send.at[0], q_recv.at[slot], device_id=(q_target(n), y), device_id_type=MESH
         )
 
     def q_start(n, carry):
@@ -155,14 +191,7 @@
 
         return carry
 
-    def q_done(n, carry):
-        @pl.when(q_target(n) != d)
-        def _():
-            q_copy(n).wait_send()
-
-        return carry
-
-    lax.fori_loop(0, CHIPS, q_start, 0)
+    lax.fori_loop(0, CHIPS, q_start, 0, unroll=True)
 
     @pl.when(home == core)
     def _():
@@ -177,7 +206,14 @@
         pvalues_t[j] = pvalues[j].T
         return carry
 
-    lax.fori_loop(0, OWN_BEAMS, turn_private, 0)
+    lax.fori_loop(0, OWN_BEAMS, turn_private, 0, unroll=True)
+    cached[1].wait()
+
+    def turn_mine(i, carry):
+        values_t[i, :, 0:256] = values[i, 0].T
+        return carry
+
+    lax.fori_loop(0, SET, turn_mine, 0, unroll=2)
     small[1].wait()
     small[2].wait()
     small[4].wait()
@@ -207,7 +243,9 @@
         pscores[j] = got
         return jnp.maximum(highest, jnp.max(got, axis=0, keepdims=True))
 
-    highest = lax.fori_loop(0, OWN_BEAMS, private_scores, jnp.max(self_scores, axis=0, keepdims=True))
+    highest = lax.fori_loop(
+        0, OWN_BEAMS, private_scores, jnp.max(self_scores, axis=0, keepdims=True), unroll=True
+    )
     weights = jnp.where(self_scores > LOWEST, jnp.exp2(self_scores - highest), 0.0)
     total = jnp.sum(weights, axis=0, keepdims=True)
     summed = jnp.dot(self_values_t, weights.astype(jnp.bfloat16), preferred_element_type=jnp.float32)
@@ -220,7 +258,7 @@
         summed = summed + jnp.dot(pvalues_t[j], weights.astype(jnp.bfloat16), preferred_element_type=jnp.float32)
         return total, summed
 
-    total, summed = lax.fori_loop(0, OWN_BEAMS, private_sums, (total, summed))
+    total, summed = lax.fori_loop(0, OWN_BEAMS, private_sums, (total, summed), unroll=True)
     num_out[SET] = summed.astype(jnp.bfloat16)
     stat_out[SET, 0:1, :] = highest
     stat_out[SET, 1:2, :] = total
@@ -233,11 +271,11 @@
             to[0] != d,
             (
                 pltpu.make_async_remote_copy(
-                    num_out.at[source, rows], num_in.at[into], num_send.at[n], num_recv.at[0],
+                    num_out.at[source, rows], num_in.at[into], num_send.at[0], num_recv.at[0],
                     device_id=to, device_id_type=MESH,
                 ),
                 pltpu.make_async_remote_copy(
-                    stat_out.at[source], stat_in.at[into], stat_send.at[n], stat_recv.at[0],
+                    stat_out.at[source], stat_in.at[into], stat_send.at[0], stat_recv.at[0],
                     device_id=to, device_id_type=MESH,
                 ),
             ),
@@ -247,8 +285,11 @@
             ),
         )
 
+    def nth_request(s):
+        return 2 * ((x + turn_x(s)) % NX) + (z // 4 + 1 + s) % 2
+
     def prompt_result(n):
-        owner_slot = (chip // 4 + n // 4) % SET
+        owner_slot = nth_request(n // 4)
         return result_copies(owner_slot, owner_slot, core, chip, n, (chip + n) % 4)
 
     def private_result(j):
@@ -267,53 +308,50 @@
             for copy in near:
                 copy.start()
 
-    def result_done(make, n):
-        remote, far, _ = make(n)
-
-        @pl.when(remote)
-        def _():
-            for copy in far:
-                copy.wait_send()
-
     def private_start(j, carry):
         result_start(private_result, j)
         return carry
 
-    lax.fori_loop(0, 4, private_start, 0)
-
-    for copy in cached:
-        copy.wait()
+    lax.fori_loop(0, 4, private_start, 0, unroll=True)
+
+    cached[0].wait()
     for copy in swaps[:2]:
         copy.wait_recv()
 
-    def turn(i, carry):
-        values_t[i] = values[i].reshape(512, HD).T
-        return carry
-
-    lax.fori_loop(0, SET, turn, 0)
-
-    def one_request(s, carry):
-        i = (chip // 4 + s) % SET
-        pltpu.make_async_copy(q_set.at[i], q_set.at[i], q_recv.at[i]).wait()
-        rows = q_set[i].reshape(128, HD)
-        scores = (
-            lax.dot_general(keys[i].reshape(512, HD), rows, LAST, preferred_element_type=jnp.float32) * TO_LOG2
-        )
-        highest = jnp.max(scores, axis=0, keepdims=True)
-        weights = jnp.exp2(scores - highest)
-        stat_out[i, 0:1, :] = highest
-        stat_out[i, 1:2, :] = jnp.sum(weights, axis=0, keepdims=True)
-        num_out[i] = jnp.dot(
-            values_t[i], weights.astype(jnp.bfloat16), preferred_element_type=jnp.float32
-        ).astype(jnp.bfloat16)
-        for j in range(4):
-            result_start(prompt_result, s * 4 + j)
-        return carry
-
-    lax.fori_loop(0, SET, one_request, 0)
-
-    lax.fori_loop(0, 4, own_done, 0)
-    lax.fori_loop(0, CHIPS, q_done, 0)
+    def turn_swapped(i, carry):
+        values_t[i, :, 256:512] = values[i, 1].T
+        return carry
+
+    lax.fori_loop(0, SET, turn_swapped, 0, unroll=2)
+
+    def two_requests(pair_at, carry):
+        some = [nth_request(pair_at * 2), nth_request(pair_at * 2 + 1)]
+        for i in some:
+            pltpu.make_async_copy(q_set.at[i], q_set.at[i], q_recv.at[i]).wait()
+        done = []
+        for i in some:
+            rows = q_set[i].reshape(128, HD)
+            scores = (
+                lax.dot_general(keys[i].reshape(512, HD), rows, LAST, preferred_element_type=jnp.float32) * TO_LOG2
+            )
+            highest = jnp.max(scores, axis=0, keepdims=True)
+            weights = jnp.exp2(scores - highest)
+            total = jnp.sum(weights, axis=0, keepdims=True)
+            summed = jnp.dot(values_t[i], weights.astype(jnp.bfloat16), preferred_element_type=jnp.float32)
+            done.append((highest, total, summed.astype(jnp.bfloat16)))
+        for i, (highest, total, summed) in zip(some, done, strict=True):
+            stat_out[i, 0:1, :] = highest
+            stat_out[i, 1:2, :] = total
+            num_out[i] = summed
+        for j in range(8):
+            result_start(prompt_result, pair_at * 8 + j)
+        return carry
+
+    lax.fori_loop(0, SET // 2, two_requests, 0, unroll=True)
+
+    sent(q_own, own_send, 3)
+    sent(par_all, par_send, 3)
+    sent_either(num_in, q_send, home == core, CHIPS)
     for copy in swaps:
         copy.wait_send()
 
@@ -346,32 +384,20 @@
     place = att_all.at[chip % 4, chip // 4]
 
     def att_copy(k):
-        to = ((((x + k // NZ) % NX) * NZ + (z + k) % NZ) * 2 + core, y)
         return pltpu.make_async_remote_copy(
-            att_mine, place, att_send.at[k], att_recv.at[0], device_id=to, device_id_type=MESH
+            att_mine, place, att_send.at[0], att_recv.at[0], device_id=same_core(k), device_id_type=MESH
         )
 
     def att_start(k, carry):
         att_copy(k).start()
         return carry
 
-    def att_done(k, carry):
-        att_copy(k).wait_send()
-        return carry
-
-    lax.fori_loop(1, CHIPS, att_start, 0)
+    lax.fori_loop(0, CHIPS - 1, att_start, 0, unroll=True)
     pltpu.make_async_copy(att_mine, place, att_recv.at[0]).start()
 
-    def prompt_done(n, carry):
-        result_done(prompt_result, n)
-        return carry
-
-    def private_done(n, carry):
-        result_done(private_result, n)
-        return carry
-
-    lax.fori_loop(0, CHIPS, prompt_done, 0)
-    lax.fori_loop(0, 4, private_done, 0)
+    kept = jnp.logical_and(home == core, chip // 4 == slot)
+    sent_either(num_in, num_send, kept, SLOTS - 1)
+    sent_either(stat_in, stat_send, kept, SLOTS - 1)
     own_weight.wait()
     swaps[2].wait_recv()
 
@@ -391,7 +417,7 @@
     def part_copy(n):
         to = part_target(n)
         return pltpu.make_async_remote_copy(
-            part.at[n % 2, (y + n // 2) % 4], part_in.at[y], part_send.at[n], part_recv.at[0],
+            part.at[n % 2, (y + n // 2) % 4], part_in.at[y], part_send.at[0], part_recv.at[0],
             device_id=to, device_id_type=MESH,
         )
 
@@ -406,26 +432,19 @@
 
         return carry
 
-    def part_done(n, carry):
-        @pl.when(part_is_far(n))
-        def _():
-            part_copy(n).wait_send()
-
-        return carry
-
-    lax.fori_loop(0, 8, part_start, 0)
+    lax.fori_loop(0, 8, part_start, 0, unroll=True)
 
     @pl.when(y // 4 == core)
     def _():
         pltpu.make_async_copy(part.at[core, y % 4], part_in.at[y], part_recv.at[0]).start()
 
-    lax.fori_loop(1, CHIPS, att_done, 0)
+    sent(num_in, att_send, CHIPS - 1)
     pltpu.make_async_copy(part_in, part_in, part_recv.at[0]).wait()
     mixed = part_in[0].astype(jnp.float32)
     for k in range(1, NY):
         mixed = mixed + part_in[k].astype(jnp.float32)
     out_ref[...] = mixed.astype(jnp.bfloat16)
-    lax.fori_loop(0, 8, part_done, 0)
+    sent_either(num_in, part_send, y // 4 == core, 8)
 
 
 def per_device(
@@ -434,6 +453,13 @@
     bf16, f32, i32 = jnp.bfloat16, jnp.float32, jnp.int32
     dma = pltpu.SemaphoreType.DMA
     anywhere = pl.BlockSpec(memory_space=pl.ANY)
+    held = [
+        pltpu.with_memory_space_constraint(operand, pltpu.HBM)
+        for operand in (
+            queries, new_keys, new_values, prompt_keys, prompt_values, private_keys, private_values, parents, counts,
+            weight.reshape(QPK, 4, 32, HD),
+        )
+    ]
     return pl.pallas_call(
         kernel,
         out_shape=jax.ShapeDtypeStruct((32, HD), bf16),
@@ -469,16 +495,13 @@
             pltpu.VMEM((2, 4, 32, HD), bf16),
             pltpu.VMEM((NY, 32, HD), bf16),
             dma((5,)), dma((2,)), dma((2,)), dma((1,)), dma((3,)), dma((3,)),
-            dma((CHIPS,)), dma((SET,)), dma((4,)), dma((1,)), dma((4,)), dma((1,)),
-            dma((SLOTS,)), dma((1,)), dma((SLOTS,)), dma((1,)), dma((CHIPS,)), dma((1,)), dma((8,)), dma((1,)),
+            dma((1,)), dma((SET,)), dma((1,)), dma((1,)), dma((1,)), dma((1,)),
+            dma((1,)), dma((1,)), dma((1,)), dma((1,)), dma((1,)), dma((1,)), dma((1,)), dma((1,)),
         ],
         compiler_params=pltpu.CompilerParams(
-            collective_id=0, has_side_effects=True, vmem_limit_bytes=48 << 20
+            collective_id=0, has_side_effects=True, vmem_limit_bytes=32 << 20
         ),
-    )(
-        queries, new_keys, new_values, prompt_keys, prompt_values, private_keys, private_values, parents, counts,
-        weight.reshape(QPK, 4, 32, HD),
-    )
+    )(*held)
 
 
 def solution(mesh):

time: 60.8 us -> 49 us (0.81)
  local copies, waits for them, and re-layouts: 8.8 us -> 0.6 us
  Pallas kernels: 51.5 us -> 48.2 us
    unnamed x21 -> x1, local copies, waits for them, and re-layouts: 8.8 us -> 0.6 us
    pallas_call x1, Pallas kernels: 51.5 us -> 48.2 us  [per_device(): pl.pallas_call(kernel, out_shape=jax.ShapeDtypeStruct((32, HD), bf16), in...]
where the time goes in v2:
time: 49 us; the launch traced here: 48.9 us
  Pallas kernels  48.2 us (98%)
  local copies, waits for them, and re-layouts  0.6 us (1%)
    pallas_call x1, Pallas kernels, per_device(): pl.pallas_call(kernel, out_shape=jax.ShapeDtypeStruct((32, HD), bf16), in...  48.2 us

profile of v2, /device:TPU:1, one launch (start us, length us, event | category | flops | bytes accessed | tf_op | source)
XLA Modules:
  0.0 48.9 jit_solution(10729305960174843325)
XLA Ops:
  0.0 48.2 %shard_map.100 = bf16[32,128]{1,0:T(8,128)(2,1)S(1)} custom-call(bf16[4,1024]{1,0:T(4,128)(2,1)} %queries.1, bf16[4,128]{1,0:T(4,128)(2,1)} %new_keys.1, bf16[4,128]{1,0:T(4,128)(2,1)} %new_values.1, bf16[16,256,128]{2,1,0:T(8,128)(2,1)} %prompt_keys.1, bf16[16,256,128]{2,1,0:T(8,128)(2,1)} %prompt_values.1, bf16[4,512,128]{2,1,0:T(8,128)(2,1)} %private_keys.1, ...), custom_call_target="tpu_custom_call" | custom-call | tf_op jit(solution)/shard_map/pallas_call | solution.py:463
  48.3 0.6 %copy.12 = bf16[32,128]{1,0:T(8,128)(2,1)} copy(bf16[32,128]{1,0:T(8,128)(2,1)S(1)} %shard_map.100) | data formatting | bytes 16384

commit v3 on v2

--- a/solution.py
+++ b/solution.py
@@ -16,7 +16,6 @@
 NX, NZ, NY = 4, 8, 8
 CHIPS = NX * NZ
 SET = 8
-SLOTS = CHIPS + 4
 TO_LOG2 = 1.0 / math.sqrt(HD) / math.log(2.0)
 LOWEST = -3.0e38
 LAST = (((1,), (1,)), ((), ()))
@@ -26,11 +25,11 @@
     queries, new_keys, new_values, prompt_keys, prompt_values, private_keys, private_values, parents, counts, weight,
     out_ref,
     q_in, nk_in, nv_in, par_in, cnt_in, q_rows, q_mine, q_set, q_own, par_mine, par_all,
-    keys, values, values_t, pkeys, pvalues, pvalues_t, self_rows, pscores, w_both,
-    num_out, stat_out, num_in, stat_in, att_mine, att_all, part, part_in,
-    small_sem, kv_sem, priv_sem, w_sem, pair_send, pair_recv,
+    keys, values, values_out, values_t, pkeys, pvalues, pvalues_t, self_rows, pscores, w_all,
+    num_out, stat_out, pair_num, pair_stat, num_in, stat_in, att_mine, att_all, part, part_in,
+    small_sem, kv_sem, priv_sem, w_sem, pair_send, pair_recv, w_send, w_recv, hand_send, hand_recv,
     q_send, q_recv, own_send, own_recv, par_send, par_recv,
-    num_send, num_recv, stat_send, stat_recv, att_send, att_recv, part_send, part_recv,
+    join_send, join_recv, num_send, num_recv, stat_send, stat_recv, att_send, att_recv, part_send, part_recv,
 ):
     d = lax.axis_index("beam")
     y = lax.axis_index("head")
@@ -72,9 +71,11 @@
         tell(((core * 16 + (chip + 8 + k) % 16) * 2 + 1 - core, y))
         return carry
 
+    from_x = jnp.where(y % 4 // 2 == x // 2, x, (x + NX - 1 + 2 * (x % 2)) % NX)
+
     def tell_column(k, carry):
         to = (y + 4 + k) % NY
-        row = chip * 2 + y // 4
+        row = (from_x * NZ + z) * 2 + y // 4
 
         @pl.when(jnp.logical_or(row != d, to != y))
         def _():
@@ -101,11 +102,11 @@
     theirs = pl.ds((1 - core) * SET, SET)
     cached = [
         pltpu.make_async_copy(prompt_keys.at[mine], keys.at[:, 0], kv_sem.at[0]),
-        pltpu.make_async_copy(prompt_values.at[mine], values.at[:, 0], kv_sem.at[1]),
+        pltpu.make_async_copy(prompt_values, values, kv_sem.at[1]),
     ]
     for copy in cached:
         copy.start()
-    own_weight = pltpu.make_async_copy(weight, w_both.at[core], w_sem.at[0])
+    own_weight = pltpu.make_async_copy(weight, w_all.at[0, core], w_sem.at[0])
     own_weight.start()
     pair = (chip * 2 + 1 - core, y)
     swaps = [
@@ -115,11 +116,21 @@
         for n, (src, dst) in enumerate(
             (
                 (prompt_keys.at[theirs], keys.at[:, 1]),
-                (prompt_values.at[theirs], values.at[:, 1]),
-                (weight, w_both.at[core]),
+                (values_out, values_t.at[:, :, pl.ds(256, 256)]),
+                (weight, w_all.at[0, core]),
             )
         )
     ]
+
+    x_pair = x + 1 - 2 * (x % 2)
+    x_next = (x + NX - 1 + 2 * (x % 2)) % NX
+    w_copy = pltpu.make_async_remote_copy(
+        weight, w_all.at[1, core], w_send.at[0], w_recv.at[0],
+        device_id=((x_next * NZ + z) * 2 + core, y), device_id_type=MESH,
+    )
+    w_hand = pltpu.make_async_remote_copy(
+        w_all.at[1, core], w_all.at[1, core], hand_send.at[0], hand_recv.at[0], device_id=pair, device_id_type=MESH
+    )
 
     small[0].wait()
     q_wide = q_in[...].astype(jnp.float32)
@@ -133,7 +144,23 @@
         row_parent = jnp.where(lane % OWN_BEAMS == beam, par_in[beam], row_parent)
     par_mine[...] = jnp.where(lane // 32 == member, row_parent, 0)
 
-    pl.semaphore_wait(barrier, jnp.where(home == core, 33, 63) + jnp.where(y // 4 == core, 7, 8))
+    private[1].wait()
+
+    def turn_private(j, carry):
+        pvalues_t[j] = pvalues[j].T
+        return carry
+
+    lax.fori_loop(0, OWN_BEAMS, turn_private, 0, unroll=True)
+    cached[1].wait()
+
+    def turn_mine(i, carry):
+        values_t[i, :, 0:256] = values[core * SET + i].T
+        values_out[i] = values[(1 - core) * SET + i].T
+        return carry
+
+    lax.fori_loop(0, SET, turn_mine, 0, unroll=2)
+    keeps = jnp.logical_and(y // 4 == core, y % 4 // 2 == x // 2)
+    pl.semaphore_wait(barrier, jnp.where(home == core, 33, 63) + jnp.where(keeps, 7, 8))
 
     def own_copy(j):
         to = (request * 4 + j, y)
@@ -170,14 +197,13 @@
     pltpu.make_async_copy(q_mine, q_own.at[member], own_recv.at[0]).start()
     pltpu.make_async_copy(par_mine, par_all.at[member], par_recv.at[0]).start()
 
-    def turn_x(s):
-        u = s // 2
-        return (2 + (u + 1) // 2 * (1 - 2 * (u % 2))) % NX
+    def nth_request(s):
+        t = s // 2
+        return (z // 2 + (t + 1) // 2 * (1 - 2 * (t % 2)) + 4) % 4 + 4 * (s % 2)
 
     def q_target(n):
-        to_x = (slot // 2 - turn_x(n // 4) + NX) % NX
-        to_z = 4 * ((slot + 1 + n // 4) % 2) + (z + n) % 4
-        return (to_x * NZ + to_z) * 2 + home
+        dx, dz = far_first(CHIPS - 1 - n)
+        return (((x + dx) % NX) * NZ + (z + dz) % NZ) * 2 + home
 
     def q_copy(n):
         return pltpu.make_async_remote_copy(
@@ -199,21 +225,8 @@
 
     for copy in swaps:
         copy.start()
-
-    private[1].wait()
-
-    def turn_private(j, carry):
-        pvalues_t[j] = pvalues[j].T
-        return carry
-
-    lax.fori_loop(0, OWN_BEAMS, turn_private, 0, unroll=True)
-    cached[1].wait()
-
-    def turn_mine(i, carry):
-        values_t[i, :, 0:256] = values[i, 0].T
-        return carry
-
-    lax.fori_loop(0, SET, turn_mine, 0, unroll=2)
+    w_copy.start()
+
     small[1].wait()
     small[2].wait()
     small[4].wait()
@@ -263,40 +276,44 @@
     stat_out[SET, 0:1, :] = highest
     stat_out[SET, 1:2, :] = total
 
-    def result_copies(source, owner_slot, to_core, into, n, quarter):
-        owner = 4 * owner_slot + quarter
+    joins = [
+        pltpu.make_async_remote_copy(
+            src, dst, join_send.at[n], join_recv.at[n], device_id=pair, device_id_type=MESH
+        )
+        for n, (src, dst) in enumerate(((num_out.at[SET], pair_num), (stat_out.at[SET], pair_stat)))
+    ]
+
+    @pl.when(home != core)
+    def _():
+        for copy in joins:
+            copy.start()
+
+    def result_copies(n):
+        i = nth_request(n // 4)
+        quarter = (x % 2 * 2 + z % 2 + n) % 4
         rows = pl.ds(pl.multiple_of(quarter * 32, 32), 32)
-        to = (owner * 2 + to_core, y)
+        owner = (i // 4 * 2 + quarter // 2) * NZ + (2 * (i % 4) + 4 + quarter % 2) % NZ
+        to = (owner * 2 + core, y)
         return (
             to[0] != d,
             (
                 pltpu.make_async_remote_copy(
-                    num_out.at[source, rows], num_in.at[into], num_send.at[0], num_recv.at[0],
+                    num_out.at[i, rows], num_in.at[chip], num_send.at[0], num_recv.at[0],
                     device_id=to, device_id_type=MESH,
                 ),
                 pltpu.make_async_remote_copy(
-                    stat_out.at[source], stat_in.at[into], stat_send.at[0], stat_recv.at[0],
+                    stat_out.at[i], stat_in.at[chip], stat_send.at[0], stat_recv.at[0],
                     device_id=to, device_id_type=MESH,
                 ),
             ),
             (
-                pltpu.make_async_copy(num_out.at[source, rows], num_in.at[into], num_recv.at[0]),
-                pltpu.make_async_copy(stat_out.at[source], stat_in.at[into], stat_recv.at[0]),
+                pltpu.make_async_copy(num_out.at[i, rows], num_in.at[chip], num_recv.at[0]),
+                pltpu.make_async_copy(stat_out.at[i], stat_in.at[chip], stat_recv.at[0]),
             ),
         )
 
-    def nth_request(s):
-        return 2 * ((x + turn_x(s)) % NX) + (z // 4 + 1 + s) % 2
-
-    def prompt_result(n):
-        owner_slot = nth_request(n // 4)
-        return result_copies(owner_slot, owner_slot, core, chip, n, (chip + n) % 4)
-
-    def private_result(j):
-        return result_copies(SET, slot, home, CHIPS + member, CHIPS + j, (chip + j) % 4)
-
-    def result_start(make, n):
-        remote, far, near = make(n)
+    def result_start(n):
+        remote, far, near = result_copies(n)
 
         @pl.when(remote)
         def _():
@@ -307,22 +324,10 @@
         def _():
             for copy in near:
                 copy.start()
-
-    def private_start(j, carry):
-        result_start(private_result, j)
-        return carry
-
-    lax.fori_loop(0, 4, private_start, 0, unroll=True)
 
     cached[0].wait()
     for copy in swaps[:2]:
         copy.wait_recv()
-
-    def turn_swapped(i, carry):
-        values_t[i, :, 256:512] = values[i, 1].T
-        return carry
-
-    lax.fori_loop(0, SET, turn_swapped, 0, unroll=2)
 
     def two_requests(pair_at, carry):
         some = [nth_request(pair_at * 2), nth_request(pair_at * 2 + 1)]
@@ -338,13 +343,33 @@
             weights = jnp.exp2(scores - highest)
             total = jnp.sum(weights, axis=0, keepdims=True)
             summed = jnp.dot(values_t[i], weights.astype(jnp.bfloat16), preferred_element_type=jnp.float32)
-            done.append((highest, total, summed.astype(jnp.bfloat16)))
+            done.append((highest, total, summed))
         for i, (highest, total, summed) in zip(some, done, strict=True):
             stat_out[i, 0:1, :] = highest
             stat_out[i, 1:2, :] = total
-            num_out[i] = summed
+            num_out[i] = summed.astype(jnp.bfloat16)
+
+            @pl.when(jnp.logical_and(home == core, i == slot))
+            def _(i=i, highest=highest, total=total, summed=summed):
+                for copy in joins:
+                    copy.wait_recv()
+                others = (
+                    (stat_out[SET, 0:1, :], stat_out[SET, 1:2, :], num_out[SET]),
+                    (pair_stat[0:1, :], pair_stat[1:2, :], pair_num[...]),
+                )
+                top = jnp.maximum(jnp.maximum(highest, others[0][0]), others[1][0])
+                share = jnp.exp2(highest - top)
+                total, summed = share * total, share * summed
+                for other_highest, other_total, other_summed in others:
+                    share = jnp.exp2(other_highest - top)
+                    total = total + share * other_total
+                    summed = summed + share * other_summed.astype(jnp.float32)
+                stat_out[i, 0:1, :] = top
+                stat_out[i, 1:2, :] = total
+                num_out[i] = summed.astype(jnp.bfloat16)
+
         for j in range(8):
-            result_start(prompt_result, pair_at * 8 + j)
+            result_start(pair_at * 8 + j)
         return carry
 
     lax.fori_loop(0, SET // 2, two_requests, 0, unroll=True)
@@ -356,17 +381,17 @@
         copy.wait_send()
 
     pltpu.make_async_copy(stat_in, stat_in, stat_recv.at[0]).wait()
-    stats = [stat_in[k] for k in range(SLOTS)]
+    stats = [stat_in[k] for k in range(CHIPS)]
     highest = stats[0][0:1, :]
-    for k in range(1, SLOTS):
+    for k in range(1, CHIPS):
         highest = jnp.maximum(highest, stats[k][0:1, :])
-    shares = [jnp.exp2(stats[k][0:1, :] - highest) for k in range(SLOTS)]
+    shares = [jnp.exp2(stats[k][0:1, :] - highest) for k in range(CHIPS)]
     total = shares[0] * stats[0][1:2, :]
-    for k in range(1, SLOTS):
+    for k in range(1, CHIPS):
         total = total + shares[k] * stats[k][1:2, :]
     pltpu.make_async_copy(num_in, num_in, num_recv.at[0]).wait()
     summed = shares[0] * num_in[0].astype(jnp.float32)
-    for k in range(1, SLOTS):
+    for k in range(1, CHIPS):
         summed = summed + shares[k] * num_in[k].astype(jnp.float32)
     attended = (summed / total).astype(jnp.bfloat16).astype(jnp.float32)
 
@@ -381,44 +406,60 @@
         chosen.astype(jnp.bfloat16), spread, LAST, preferred_element_type=jnp.float32
     ).astype(jnp.bfloat16)
 
-    place = att_all.at[chip % 4, chip // 4]
+
+    place = att_all.at[x % 2 * 2 + z % 2, (z // 2 + 2) % 4]
 
     def att_copy(k):
+        to_x = jnp.where(k % 2 == 0, x_pair, x)
+        to = ((to_x * NZ + (z + far_first(2 * k - 2 * (k % 2))[1]) % NZ) * 2 + core, y)
         return pltpu.make_async_remote_copy(
-            att_mine, place, att_send.at[0], att_recv.at[0], device_id=same_core(k), device_id_type=MESH
+            att_mine, place, att_send.at[0], att_recv.at[0], device_id=to, device_id_type=MESH
         )
 
     def att_start(k, carry):
         att_copy(k).start()
         return carry
 
-    lax.fori_loop(0, CHIPS - 1, att_start, 0, unroll=True)
+    lax.fori_loop(0, 2 * NZ - 1, att_start, 0, unroll=True)
     pltpu.make_async_copy(att_mine, place, att_recv.at[0]).start()
 
-    kept = jnp.logical_and(home == core, chip // 4 == slot)
-    sent_either(num_in, num_send, kept, SLOTS - 1)
-    sent_either(stat_in, stat_send, kept, SLOTS - 1)
+    sent(num_in, num_send, CHIPS - 1)
+    sent(stat_in, stat_send, CHIPS - 1)
+
+    @pl.when(home != core)
+    def _():
+        for copy in joins:
+            copy.wait_send()
+
     own_weight.wait()
+    w_copy.wait_recv()
+    w_hand.start()
     swaps[2].wait_recv()
 
     pltpu.make_async_copy(att_all, att_all, att_recv.at[0]).wait()
-    rows = [att_all[quarter].reshape(128, 256) for quarter in range(4)]
-    for side in range(2):
-        product = jnp.zeros((128, HD), jnp.float32)
+    w_hand.wait_recv()
+    rows = [att_all[quarter].reshape(64, 256) for quarter in range(4)]
+
+    def project(n, carry):
+        product = jnp.zeros((64, HD), jnp.float32)
         for quarter in range(4):
             product = product + jnp.dot(
-                rows[quarter], w_both[side, :, quarter].reshape(256, HD), preferred_element_type=jnp.float32
+                rows[quarter], w_all[n // 2, n % 2, :, quarter].reshape(256, HD), preferred_element_type=jnp.float32
             )
-        part[side] = product.astype(jnp.bfloat16).reshape(4, 32, HD)
+        part[n // 2, n % 2] = product.astype(jnp.bfloat16).reshape(2, 32, HD)
+        return carry
+
+    lax.fori_loop(0, 4, project, 0, unroll=True)
 
     def part_target(n):
-        return chip * 2 + n % 2, core * 4 + (y + n // 2) % 4
+        to_x = jnp.where(n // 4 == 0, x_next, x)
+        to_y = core * 4 + x // 2 * 2 + n % 2
+        return (to_x * NZ + z) * 2 + n // 2 % 2, to_y
 
     def part_copy(n):
-        to = part_target(n)
         return pltpu.make_async_remote_copy(
-            part.at[n % 2, (y + n // 2) % 4], part_in.at[y], part_send.at[0], part_recv.at[0],
-            device_id=to, device_id_type=MESH,
+            part.at[1 - n // 4, n // 2 % 2, n % 2], part_in.at[y], part_send.at[0], part_recv.at[0],
+            device_id=part_target(n), device_id_type=MESH,
         )
 
     def part_is_far(n):
@@ -434,17 +475,21 @@
 
     lax.fori_loop(0, 8, part_start, 0, unroll=True)
 
-    @pl.when(y // 4 == core)
+    @pl.when(keeps)
     def _():
-        pltpu.make_async_copy(part.at[core, y % 4], part_in.at[y], part_recv.at[0]).start()
-
-    sent(num_in, att_send, CHIPS - 1)
+        pltpu.make_async_copy(
+            part.at[0, core, y % 2], part_in.at[y], part_recv.at[0]
+        ).start()
+
+    sent(num_in, att_send, 2 * NZ - 1)
     pltpu.make_async_copy(part_in, part_in, part_recv.at[0]).wait()
     mixed = part_in[0].astype(jnp.float32)
     for k in range(1, NY):
         mixed = mixed + part_in[k].astype(jnp.float32)
     out_ref[...] = mixed.astype(jnp.bfloat16)
-    sent_either(num_in, part_send, y // 4 == core, 8)
+    sent_either(num_in, part_send, keeps, 8)
+    w_copy.wait_send()
+    w_hand.wait_send()
 
 
 def per_device(
@@ -478,25 +523,28 @@
             pltpu.VMEM((8, HD), i32),
             pltpu.VMEM((4, 8, HD), i32),
             pltpu.VMEM((SET, 2, 256, HD), bf16),
-            pltpu.VMEM((SET, 2, 256, HD), bf16),
+            pltpu.VMEM((2 * SET, 256, HD), bf16),
+            pltpu.VMEM((SET, HD, 256), bf16),
             pltpu.VMEM((SET, HD, 512), bf16),
             pltpu.VMEM((OWN_BEAMS, PRIV, HD), bf16),
             pltpu.VMEM((OWN_BEAMS, PRIV, HD), bf16),
             pltpu.VMEM((OWN_BEAMS, HD, PRIV), bf16),
             pltpu.VMEM((2, HD, HD), f32),
             pltpu.VMEM((OWN_BEAMS, PRIV, HD), f32),
-            pltpu.VMEM((2, QPK, 4, 32, HD), bf16),
+            pltpu.VMEM((2, 2, QPK, 4, 32, HD), bf16),
             pltpu.VMEM((SET + 1, HD, HD), bf16),
             pltpu.VMEM((SET + 1, 2, HD), f32),
-            pltpu.VMEM((SLOTS, 32, HD), bf16),
-            pltpu.VMEM((SLOTS, 2, HD), f32),
+            pltpu.VMEM((HD, HD), bf16),
+            pltpu.VMEM((2, HD), f32),
+            pltpu.VMEM((CHIPS, 32, HD), bf16),
+            pltpu.VMEM((CHIPS, 2, HD), f32),
             pltpu.VMEM((16, 256), bf16),
-            pltpu.VMEM((4, SET, 16, 256), bf16),
-            pltpu.VMEM((2, 4, 32, HD), bf16),
+            pltpu.VMEM((4, 4, 16, 256), bf16),
+            pltpu.VMEM((2, 2, 2, 32, HD), bf16),
             pltpu.VMEM((NY, 32, HD), bf16),
-            dma((5,)), dma((2,)), dma((2,)), dma((1,)), dma((3,)), dma((3,)),
+            dma((5,)), dma((2,)), dma((2,)), dma((1,)), dma((3,)), dma((3,)), dma((1,)), dma((1,)), dma((1,)), dma((1,)),
             dma((1,)), dma((SET,)), dma((1,)), dma((1,)), dma((1,)), dma((1,)),
-            dma((1,)), dma((1,)), dma((1,)), dma((1,)), dma((1,)), dma((1,)), dma((1,)), dma((1,)),
+            dma((2,)), dma((2,)), dma((1,)), dma((1,)), dma((1,)), dma((1,)), dma((1,)), dma((1,)), dma((1,)), dma((1,)),
         ],
         compiler_params=pltpu.CompilerParams(
             collective_id=0, has_side_effects=True, vmem_limit_bytes=32 << 20

time: 49 us -> 46.3 us (0.945)
  Pallas kernels: 48.2 us -> 45.5 us
    pallas_call x1, Pallas kernels: 48.2 us -> 45.5 us  [per_device(): pl.pallas_call(kernel, out_shape=jax.ShapeDtypeStruct((32, HD), bf16), in...]
where the time goes in v3:
time: 46.3 us; the launch traced here: 46.1 us
  Pallas kernels  45.5 us (98%)
  local copies, waits for them, and re-layouts  0.6 us (1%)
    pallas_call x1, Pallas kernels, per_device(): pl.pallas_call(kernel, out_shape=jax.ShapeDtypeStruct((32, HD), bf16), in...  45.5 us

profile of v3, /device:TPU:1, one launch (start us, length us, event | category | flops | bytes accessed | tf_op | source)
XLA Modules:
  0.0 46.1 jit_solution(17542710065830185213)
XLA Ops:
  0.0 45.5 %shard_map.100 = bf16[32,128]{1,0:T(8,128)(2,1)S(1)} custom-call(bf16[4,1024]{1,0:T(4,128)(2,1)} %queries.1, bf16[4,128]{1,0:T(4,128)(2,1)} %new_keys.1, bf16[4,128]{1,0:T(4,128)(2,1)} %new_values.1, bf16[16,256,128]{2,1,0:T(8,128)(2,1)} %prompt_keys.1, bf16[16,256,128]{2,1,0:T(8,128)(2,1)} %prompt_values.1, bf16[4,512,128]{2,1,0:T(8,128)(2,1)} %private_keys.1, ...), custom_call_target="tpu_custom_call" | custom-call | tf_op jit(solution)/shard_map/pallas_call | solution.py:508
  45.5 0.6 %copy.12 = bf16[32,128]{1,0:T(8,128)(2,1)} copy(bf16[32,128]{1,0:T(8,128)(2,1)S(1)} %shard_map.100) | data formatting | bytes 16384

commit v4 on v3

--- a/solution.py
+++ b/solution.py
@@ -15,6 +15,7 @@
 PRIV = 512
 NX, NZ, NY = 4, 8, 8
 CHIPS = NX * NZ
+DIRECT = 20
 SET = 8
 TO_LOG2 = 1.0 / math.sqrt(HD) / math.log(2.0)
 LOWEST = -3.0e38
@@ -26,9 +27,9 @@
     out_ref,
     q_in, nk_in, nv_in, par_in, cnt_in, q_rows, q_mine, q_set, q_own, par_mine, par_all,
     keys, values, values_out, values_t, pkeys, pvalues, pvalues_t, self_rows, pscores, w_all,
-    num_out, stat_out, pair_num, pair_stat, num_in, stat_in, att_mine, att_all, part, part_in,
+    private_num, num_out, stat_out, pair_num, pair_stat, num_in, stat_in, att_mine, att_all, part, part_in,
     small_sem, kv_sem, priv_sem, w_sem, pair_send, pair_recv, w_send, w_recv, hand_send, hand_recv,
-    q_send, q_recv, own_send, own_recv, par_send, par_recv,
+    relay_send, q_send, q_recv, own_send, own_recv, par_send, par_recv,
     join_send, join_recv, num_send, num_recv, stat_send, stat_recv, att_send, att_recv, part_send, part_recv,
 ):
     d = lax.axis_index("beam")
@@ -199,11 +200,15 @@
 
     def nth_request(s):
         t = s // 2
-        return (z // 2 + (t + 1) // 2 * (1 - 2 * (t % 2)) + 4) % 4 + 4 * (s % 2)
+        side = (1 - 2 * (t % 2)) * (1 - 2 * (z % 2))
+        return (z // 2 + (t + 1) // 2 * side + 4) % 4 + 4 * (s % 2)
 
     def q_target(n):
-        dx, dz = far_first(CHIPS - 1 - n)
-        return (((x + dx) % NX) * NZ + (z + dz) % NZ) * 2 + home
+        rest = n - NZ
+        near_z = (z + far_first((CHIPS - 4 - 4 * n + CHIPS * 4) % CHIPS)[1]) % NZ
+        to_x = jnp.where(n < NZ, x, (x + 1 + rest % 6 // 2) % NX)
+        to_z = jnp.where(n < NZ, near_z, (z // 2 * 2 + rest // 6 * 4 + rest % 2) % NZ)
+        return (to_x * NZ + to_z) * 2 + home
 
     def q_copy(n):
         return pltpu.make_async_remote_copy(
@@ -217,7 +222,7 @@
 
         return carry
 
-    lax.fori_loop(0, CHIPS, q_start, 0, unroll=True)
+    lax.fori_loop(0, DIRECT, q_start, 0, unroll=True)
 
     @pl.when(home == core)
     def _():
@@ -225,7 +230,6 @@
 
     for copy in swaps:
         copy.start()
-    w_copy.start()
 
     small[1].wait()
     small[2].wait()
@@ -239,6 +243,16 @@
     private[0].wait()
     pltpu.make_async_copy(q_own, q_own, own_recv.at[0]).wait()
     pltpu.make_async_copy(par_all, par_all, par_recv.at[0]).wait()
+
+    def relay(t):
+        i = nth_request(2 * t + x % 2)
+        pltpu.make_async_copy(q_set.at[i], q_set.at[i], q_recv.at[i]).wait()
+        for dx in (2, 1, 3):
+            pltpu.make_async_remote_copy(
+                q_set.at[i], q_set.at[i], relay_send.at[t - 1], q_recv.at[i],
+                device_id=((((x + dx) % NX) * NZ + z) * 2 + core, y), device_id_type=MESH,
+            ).start()
+
     q_request = q_own[...].reshape(128, HD)
     row_parent = par_all[0] + par_all[1] + par_all[2] + par_all[3]
     row_parent = row_parent[0:1, :]
@@ -272,7 +286,7 @@
         return total, summed
 
     total, summed = lax.fori_loop(0, OWN_BEAMS, private_sums, (total, summed), unroll=True)
-    num_out[SET] = summed.astype(jnp.bfloat16)
+    private_num[...] = summed
     stat_out[SET, 0:1, :] = highest
     stat_out[SET, 1:2, :] = total
 
@@ -280,13 +294,18 @@
         pltpu.make_async_remote_copy(
             src, dst, join_send.at[n], join_recv.at[n], device_id=pair, device_id_type=MESH
         )
-        for n, (src, dst) in enumerate(((num_out.at[SET], pair_num), (stat_out.at[SET], pair_stat)))
+        for n, (src, dst) in enumerate(((private_num, pair_num), (stat_out.at[SET], pair_stat)))
     ]
 
     @pl.when(home != core)
     def _():
         for copy in joins:
             copy.start()
+
+    @pl.when(home == core)
+    def _():
+        relay(1)
+        relay(2)
 
     def result_copies(n):
         i = nth_request(n // 4)
@@ -331,8 +350,12 @@
 
     def two_requests(pair_at, carry):
         some = [nth_request(pair_at * 2), nth_request(pair_at * 2 + 1)]
-        for i in some:
-            pltpu.make_async_copy(q_set.at[i], q_set.at[i], q_recv.at[i]).wait()
+        for side, i in enumerate(some):
+
+            @pl.when(jnp.logical_not(jnp.logical_and(jnp.logical_and(home == core, side == x % 2), pair_at % 3 != 0)))
+            def _(i=i):
+                pltpu.make_async_copy(q_set.at[i], q_set.at[i], q_recv.at[i]).wait()
+
         done = []
         for i in some:
             rows = q_set[i].reshape(128, HD)
@@ -354,7 +377,7 @@
                 for copy in joins:
                     copy.wait_recv()
                 others = (
-                    (stat_out[SET, 0:1, :], stat_out[SET, 1:2, :], num_out[SET]),
+                    (stat_out[SET, 0:1, :], stat_out[SET, 1:2, :], private_num[...]),
                     (pair_stat[0:1, :], pair_stat[1:2, :], pair_num[...]),
                 )
                 top = jnp.maximum(jnp.maximum(highest, others[0][0]), others[1][0])
@@ -363,7 +386,7 @@
                 for other_highest, other_total, other_summed in others:
                     share = jnp.exp2(other_highest - top)
                     total = total + share * other_total
-                    summed = summed + share * other_summed.astype(jnp.float32)
+                    summed = summed + share * other_summed
                 stat_out[i, 0:1, :] = top
                 stat_out[i, 1:2, :] = total
                 num_out[i] = summed.astype(jnp.bfloat16)
@@ -373,10 +396,17 @@
         return carry
 
     lax.fori_loop(0, SET // 2, two_requests, 0, unroll=True)
+    w_copy.start()
 
     sent(q_own, own_send, 3)
     sent(par_all, par_send, 3)
-    sent_either(num_in, q_send, home == core, CHIPS)
+    sent_either(num_in, q_send, home == core, DIRECT)
+
+    @pl.when(home == core)
+    def _():
+        for t in range(2):
+            pltpu.make_async_copy(num_in.at[pl.ds(0, 12)], num_in.at[pl.ds(0, 12)], relay_send.at[t]).wait()
+
     for copy in swaps:
         copy.wait_send()
 
@@ -532,9 +562,10 @@
             pltpu.VMEM((2, HD, HD), f32),
             pltpu.VMEM((OWN_BEAMS, PRIV, HD), f32),
             pltpu.VMEM((2, 2, QPK, 4, 32, HD), bf16),
-            pltpu.VMEM((SET + 1, HD, HD), bf16),
+            pltpu.VMEM((HD, HD), f32),
+            pltpu.VMEM((SET, HD, HD), bf16),
             pltpu.VMEM((SET + 1, 2, HD), f32),
-            pltpu.VMEM((HD, HD), bf16),
+            pltpu.VMEM((HD, HD), f32),
             pltpu.VMEM((2, HD), f32),
             pltpu.VMEM((CHIPS, 32, HD), bf16),
             pltpu.VMEM((CHIPS, 2, HD), f32),
@@ -543,7 +574,7 @@
             pltpu.VMEM((2, 2, 2, 32, HD), bf16),
             pltpu.VMEM((NY, 32, HD), bf16),
             dma((5,)), dma((2,)), dma((2,)), dma((1,)), dma((3,)), dma((3,)), dma((1,)), dma((1,)), dma((1,)), dma((1,)),
-            dma((1,)), dma((SET,)), dma((1,)), dma((1,)), dma((1,)), dma((1,)),
+            dma((2,)), dma((1,)), dma((SET,)), dma((1,)), dma((1,)), dma((1,)), dma((1,)),
             dma((2,)), dma((2,)), dma((1,)), dma((1,)), dma((1,)), dma((1,)), dma((1,)), dma((1,)), dma((1,)), dma((1,)),
         ],
         compiler_params=pltpu.CompilerParams(

time: 46.3 us -> 45 us (0.972)
  Pallas kernels: 45.5 us -> 44.1 us
    pallas_call x1, Pallas kernels: 45.5 us -> 44.1 us  [per_device(): pl.pallas_call(kernel, out_shape=jax.ShapeDtypeStruct((32, HD), bf16), in...]
where the time goes in v4:
time: 45 us; the launch traced here: 44.7 us
  Pallas kernels  44.1 us (98%)
  local copies, waits for them, and re-layouts  0.6 us (1%)
    pallas_call x1, Pallas kernels, per_device(): pl.pallas_call(kernel, out_shape=jax.ShapeDtypeStruct((32, HD), bf16), in...  44.1 us

profile of v4, /device:TPU:1, one launch (start us, length us, event | category | flops | bytes accessed | tf_op | source)
XLA Modules:
  0.0 44.7 jit_solution(9516139527761558000)
XLA Ops:
  0.0 44.1 %shard_map.100 = bf16[32,128]{1,0:T(8,128)(2,1)S(1)} custom-call(bf16[4,1024]{1,0:T(4,128)(2,1)} %queries.1, bf16[4,128]{1,0:T(4,128)(2,1)} %new_keys.1, bf16[4,128]{1,0:T(4,128)(2,1)} %new_values.1, bf16[16,256,128]{2,1,0:T(8,128)(2,1)} %prompt_keys.1, bf16[16,256,128]{2,1,0:T(8,128)(2,1)} %prompt_values.1, bf16[4,512,128]{2,1,0:T(8,128)(2,1)} %private_keys.1, ...), custom_call_target="tpu_custom_call" | custom-call | tf_op jit(solution)/shard_map/pallas_call | solution.py:538
  44.1 0.6 %copy.12 = bf16[32,128]{1,0:T(8,128)(2,1)} copy(bf16[32,128]{1,0:T(8,128)(2,1)S(1)} %shard_map.100) | data formatting | bytes 16384

commit v5 on v4

--- a/solution.py
+++ b/solution.py
@@ -69,7 +69,8 @@
         return carry
 
     def tell_other(k, carry):
-        tell(((core * 16 + (chip + 8 + k) % 16) * 2 + 1 - core, y))
+        dz = far_first(k // 2 * 4)[1]
+        tell((((core * 2 + k % 2) * NZ + (z + dz) % NZ) * 2 + 1 - core, y))
         return carry
 
     from_x = jnp.where(y % 4 // 2 == x // 2, x, (x + NX - 1 + 2 * (x % 2)) % NX)
@@ -84,8 +85,10 @@
 
         return carry
 
-    lax.fori_loop(0, CHIPS - 1, tell_same, 0, unroll=True)
-    lax.fori_loop(0, 16, tell_other, 0, unroll=True)
+    lax.fori_loop(0, 16, tell_same, 0, unroll=True)
+    lax.fori_loop(0, 8, tell_other, 0, unroll=True)
+    lax.fori_loop(16, CHIPS - 1, tell_same, 0, unroll=True)
+    lax.fori_loop(8, 16, tell_other, 0, unroll=True)
     lax.fori_loop(0, NY, tell_column, 0, unroll=True)
 
     @pl.when(home != core)
@@ -440,8 +443,8 @@
     place = att_all.at[x % 2 * 2 + z % 2, (z // 2 + 2) % 4]
 
     def att_copy(k):
-        to_x = jnp.where(k % 2 == 0, x_pair, x)
-        to = ((to_x * NZ + (z + far_first(2 * k - 2 * (k % 2))[1]) % NZ) * 2 + core, y)
+        to_x = jnp.where(k < NZ, x_pair, x)
+        to = ((to_x * NZ + (z + far_first(k % NZ * 4)[1]) % NZ) * 2 + core, y)
         return pltpu.make_async_remote_copy(
             att_mine, place, att_send.at[0], att_recv.at[0], device_id=to, device_id_type=MESH
         )

time: 45 us -> 44.9 us (level)
  no operation moved by 1% of the time
where the time goes in v5:
time: 44.9 us; the launch traced here: 44.7 us
  Pallas kernels  44 us (98%)
  local copies, waits for them, and re-layouts  0.6 us (1%)
    pallas_call x1, Pallas kernels, per_device(): pl.pallas_call(kernel, out_shape=jax.ShapeDtypeStruct((32, HD), bf16), in...  44 us

profile of v5, /device:TPU:1, one launch (start us, length us, event | category | flops | bytes accessed | tf_op | source)
XLA Modules:
  0.0 44.7 jit_solution(13141104152560401649)
XLA Ops:
  0.0 44.0 %shard_map.100 = bf16[32,128]{1,0:T(8,128)(2,1)S(1)} custom-call(bf16[4,1024]{1,0:T(4,128)(2,1)} %queries.1, bf16[4,128]{1,0:T(4,128)(2,1)} %new_keys.1, bf16[4,128]{1,0:T(4,128)(2,1)} %new_values.1, bf16[16,256,128]{2,1,0:T(8,128)(2,1)} %prompt_keys.1, bf16[16,256,128]{2,1,0:T(8,128)(2,1)} %prompt_values.1, bf16[4,512,128]{2,1,0:T(8,128)(2,1)} %private_keys.1, ...), custom_call_target="tpu_custom_call" | custom-call | tf_op jit(solution)/shard_map/pallas_call | solution.py:541
  44.0 0.6 %copy.12 = bf16[32,128]{1,0:T(8,128)(2,1)} copy(bf16[32,128]{1,0:T(8,128)(2,1)S(1)} %shard_map.100) | data formatting | bytes 16384

commit v6 on v5

--- a/solution.py
+++ b/solution.py
@@ -69,8 +69,12 @@
         return carry
 
     def tell_other(k, carry):
-        dz = far_first(k // 2 * 4)[1]
-        tell((((core * 2 + k % 2) * NZ + (z + dz) % NZ) * 2 + 1 - core, y))
+        to_x, to_z = core * 2 + k % 2, (z + far_first(k // 2 * 4)[1]) % NZ
+
+        @pl.when(jnp.logical_or(to_x == x, to_z // 2 % 2 == z // 2 % 2))
+        def _():
+            tell(((to_x * NZ + to_z) * 2 + 1 - core, y))
+
         return carry
 
     from_x = jnp.where(y % 4 // 2 == x // 2, x, (x + NX - 1 + 2 * (x % 2)) % NX)
@@ -164,7 +168,7 @@
 
     lax.fori_loop(0, SET, turn_mine, 0, unroll=2)
     keeps = jnp.logical_and(y // 4 == core, y % 4 // 2 == x // 2)
-    pl.semaphore_wait(barrier, jnp.where(home == core, 33, 63) + jnp.where(keeps, 7, 8))
+    pl.semaphore_wait(barrier, jnp.where(home == core, 33, 51) + jnp.where(keeps, 7, 8))
 
     def own_copy(j):
         to = (request * 4 + j, y)

time: 44.9 us -> 45 us (level)
  no operation moved by 1% of the time
where the time goes in v6:
time: 45 us; the launch traced here: 44.6 us
  Pallas kernels  44 us (98%)
  local copies, waits for them, and re-layouts  0.6 us (1%)
    pallas_call x1, Pallas kernels, per_device(): pl.pallas_call(kernel, out_shape=jax.ShapeDtypeStruct((32, HD), bf16), in...  44 us

profile of v6, /device:TPU:1, one launch (start us, length us, event | category | flops | bytes accessed | tf_op | source)
XLA Modules:
  0.0 44.6 jit_solution(16644104494073606286)
XLA Ops:
  0.0 44.0 %shard_map.100 = bf16[32,128]{1,0:T(8,128)(2,1)S(1)} custom-call(bf16[4,1024]{1,0:T(4,128)(2,1)} %queries.1, bf16[4,128]{1,0:T(4,128)(2,1)} %new_keys.1, bf16[4,128]{1,0:T(4,128)(2,1)} %new_values.1, bf16[16,256,128]{2,1,0:T(8,128)(2,1)} %prompt_keys.1, bf16[16,256,128]{2,1,0:T(8,128)(2,1)} %prompt_values.1, bf16[4,512,128]{2,1,0:T(8,128)(2,1)} %private_keys.1, ...), custom_call_target="tpu_custom_call" | custom-call | tf_op jit(solution)/shard_map/pallas_call | solution.py:545
  44.0 0.6 %copy.12 = bf16[32,128]{1,0:T(8,128)(2,1)} copy(bf16[32,128]{1,0:T(8,128)(2,1)S(1)} %shard_map.100) | data formatting | bytes 16384
